TPU v7x, 256 devices: a whole 4x4x8 slice. The times are simulated.
256 devices in a mesh: tile: 8 (over z_lo, y), epoch: 32 (over x, z_hi, core).
Axes of the slice: x: 4, y: 4, z: 8 (z_hi: 4, z_lo: 2; z = z_hi * 2 + z_lo), core: 2. Of those that a mesh axis runs over, the one named last changes fastest.
Arguments:
- scene: float32 [2, 256, 1024], P(None, 'epoch', 'tile'), may hold values from -6 to 6
- kernels_h: float32 [64, 2, 5, 21], P('epoch'), may hold values from -1.25 to 1.25
- kernels_v: float32 [64, 2, 5, 21], P('epoch'), may hold values from -1.25 to 1.25
- coeffs: bfloat16 [64, 5, 256, 1024], P('epoch', None, None, 'tile'), may hold values from -2.5 to 2.5
- observed: bfloat16 [64, 2, 256, 1024], P('epoch', None, None, 'tile'), may hold values from -6 to 6
- good_pixels: int32 [64, 256, 1024], P('epoch', None, 'tile'), may hold values 0 or 1
- coverage: int32 [64, 8], P('epoch', 'tile'), may hold values 0 or 1
- offsets: int32 [64, 8, 2], P('epoch', 'tile'), may hold values from -8 to 8, as said below
Outputs:
- scene_grad: float32 [2, 256, 1024], P(None, 'epoch', 'tile')
Inputs may be any that keep to these rules, and one draw needn't show every extreme that they name: offsets[e, t] = (dy, dx); every offset lies in the stated range, and both ends of it are reached in each draw.
All inputs are finite; a program needn't handle non-finite values. No bound on the sum of `good_pixels` or of `coverage` on one device may be relied on, other than what follows from the above.
Results may differ from a plain program's by a relative error of at most 0.0003.
Values sent between devices are 32-bit elements; how exact they have to be, the bound alone decides.
A program may use at most 64 MiB of HBM per device.

v0:
```python
import jax
import jax.numpy as jnp
from jax import lax
from jax.sharding import PartitionSpec as P

TAPS = 21
SHIFT = 8


def padded_2(shard, sides, width):
    for axis, dim in sides:
        count, length = (lax.axis_size(axis), shard.shape[dim])
        up = [(i, (i + 1) % count) for i in range(count - 1)]
        down = [(j, i) for i, j in up]
        last = lax.slice_in_dim(shard, length - width, length, axis=dim)
        initial = lax.slice_in_dim(shard, 0, width, axis=dim)
        before = lax.ppermute(last, axis, up)
        after = lax.ppermute(initial, axis, down)
        shard = jnp.concatenate([before, shard, after], axis=dim)
    return shard


def predict(window, horiz, vert, maps, rows, width):
    taps = horiz.shape[-1]
    across = horiz[:, :, 0, None, None] * window[:, None, :, 0:width]
    for index in range(1, taps):
        across = across + horiz[:, :, index, None, None] * window[:, None, :, index : index + width]
    down = vert[:, :, 0, None, None] * across[:, :, 0:rows, :]
    for index in range(1, taps):
        down = down + vert[:, :, index, None, None] * across[:, :, index : index + rows, :]
    return jnp.sum(down * maps[None], axis=1)


def fold_edges(inner, gotten, margin):
    width = inner.shape[2]
    from_left = jnp.pad(gotten[:, :, :margin], ((0, 0), (0, 0), (0, width - margin)))
    from_right = jnp.pad(gotten[:, :, -margin:], ((0, 0), (0, 0), (width - margin, 0)))
    return inner + from_left + from_right


def per_device(scene, kernels_h, kernels_v, coeffs, observed, good_pixels, coverage, offsets):
    bands = scene.shape[0]
    width = scene.shape[2]
    reach = (TAPS - 1) // 2
    margin = SHIFT + reach
    whole = lax.all_gather(scene, "epoch", axis=1, tiled=True)
    extended = padded_2(whole, (("tile", 2),), margin)
    rows = extended.shape[1]
    padded = jnp.pad(extended, ((0, 0), (margin, margin), (0, 0)))

    def gradient_term(items):
        horiz, vert, maps, seen, good, cover, shifts = items
        maps = maps.astype(jnp.float32)
        start_row = margin + shifts[0] - reach
        start_col = margin + shifts[1] - reach

        def model(field):
            window = lax.dynamic_slice(
                field,
                (jnp.int32(0), start_row, start_col),
                (bands, rows + 2 * reach, width + 2 * reach),
            )
            return predict(window, horiz, vert, maps, rows, width)

        image, pullback = jax.vjp(model, padded)
        weight = (good * cover).astype(jnp.float32)
        residual = weight[None] * (image - seen.astype(jnp.float32))
        (grad,) = pullback(residual)
        return grad

    def epoch_step(total, items):
        grad = gradient_term(items)
        return (total + grad, None)

    total, unused = lax.scan(
        epoch_step,
        jnp.zeros_like(padded),
        (kernels_h, kernels_v, coeffs, observed, good_pixels, coverage[:, 0], offsets[:, 0, :]),
    )
    grad_ext = total[:, margin : margin + rows, :]
    edges = jnp.concatenate((grad_ext[:, :, :margin], grad_ext[:, :, -margin:]), axis=2)
    gotten = padded_2(edges, (("tile", 2),), margin)
    inner = fold_edges(grad_ext[:, :, margin : margin + width], gotten, margin)
    return lax.psum_scatter(inner, "epoch", scatter_dimension=1, tiled=True)


def solution(mesh):
    in_specs = (
        P(None, "epoch", "tile"),
        P("epoch", None, None, None),
        P("epoch", None, None, None),
        P("epoch", None, None, "tile"),
        P("epoch", None, None, "tile"),
        P("epoch", None, "tile"),
        P("epoch", "tile"),
        P("epoch", "tile", None),
    )
    out_specs = P(None, "epoch", "tile")
    return jax.shard_map(
        per_device, mesh=mesh, in_specs=in_specs, out_specs=out_specs, check_vma=False
    )
```

profile of v0, /device:TPU:1, one launch (start us, length us, event | category | flops | bytes accessed | tf_op | source)
XLA Modules:
  0.0 500.7 jit_solution(9911697004593645653)
XLA Ops:
  6.5 0.7 copy.105
  7.2 49.3 %all_gather.3 = f32[2,256,128]{2,0,1:T(2,128)S(1)} all-gather(f32[2,8,128]{2,0,1:T(2,128)S(1)} %copy.105), channel_id=1, replica_groups=mesh['tile'=8,'epoch'=32] {'epoch'}, dimensions={1}, use_global_device_ids=true | all-gather | bytes 270336 | tf_op jit(solution)/shard_map/all_gather | solution.py:46
  56.9 3.2 collective-permute-start
  60.1 1.3 collective-permute-start.1
  61.4 4.2 collective-permute-done
  65.6 3.8 collective-permute-done.1
  69.4 0.9 select_maximum_fusion
  70.3 1.0 broadcast.123
  71.3 328.3 %while.15 = (s32[]{:T(128)}, f32[2,292,164]{2,0,1:T(2,128)}, s32[2,2]{1,0:T(2,128)S(1)}, f32[2,2,5,21]{3,1,2,0:T(2,128)S(1)}, f32[2,2,5,21]{3,1,2,0:T(2,128)S(1)...) while((s32[]{:T(128)}, f32[2,292,164]{2,0,1:T(2,128)}, ...), condition=%wide.region_23.24_spmd, body=%wide.region_0.23_spmd.sunk | while | flops 58607036 | bytes 127720728 | solution.py:75
  71.5 0.7 dynamic_slice.103
  72.2 0.6 fusion.30
  79.4 1.6 convert_bitcast_fusion.2
  81.0 1.0 bitcast_convert_fusion.2
  82.0 1.3 constant_dynamic-slice_fusion.30
  83.3 5.1 %constant_dynamic-slice_fusion.31 = (f32[2,276,128]{2,0,1:T(2,128)S(1)}, f32[2,276,128]{2,0,1:T(2,128)S(1)}, f32[2,276,128]{2,0,1:T(2,128)S(1)}, f32[2,276,128]{...) fusion(f32[2,292,164]{2,0,1:T(2,128)S(1)} %get-tuple-element.75, ...), kind=kLoop, calls=%fused_computation.111.clone.1 | loop fusion | bytes 9609288 | tf_op jit(solution)/shard_map/while/body/eval_jaxpr/jvp()/slice | solution.py:25
  88.4 10.0 %multiply_add_fusion.2 = f32[2,5,276,128]{3,0,2,1:T(2,128)S(1)} fusion(f32[2,276,128]{2,0,1:T(2,128)S(1)} %get-tuple-element.575, f32[2,276,128]{2,0,1:T(2,128)S(1)} %get-tuple-element.576, f32[2,5]{0,1:T(8,128)S(1)} %copy.165, f32[2,276,128]{2,0,1:T(2,128)S(1)} %get-tuple-element.577, f32[2,5]{0,1:T(8,128)S(1)} %copy.167, ...), kind=kLoop, calls=%fused_computation.43.clone.1 | loop fusion | flops 14484480 | bytes 7349064 | tf_op jit(solution)/shard_map/while/body/eval_jaxpr/jvp()/add | solution.py:27
  98.4 8.9 %fusion.31 = f32[2,256,128]{2,0,1:T(2,128)S(1)} fusion(f32[2,5,276,128]{3,0,2,1:T(2,128)S(1)} %multiply_add_fusion.2, f32[5,256,128]{2,1,0:T(8,128)S(1)} %bitcast_convert_fusion.2, f32[2,5]{0,1:T(8,128)S(1)} %copy.187, f32[2,5]{0,1:T(8,128)S(1)} %copy.188, f32[2,5]{0,1:T(8,128)S(1)} %copy.189, f32[2,5]{0,1:T(8,128)S(1)} %copy.190, ...), kind=kLoop, calls=%fused_computation.86.clone.1 | loop fusion | flops 14024704 | bytes 28443464 | tf_op jit(solution)/shard_map/while/body/eval_jaxpr/jvp()/reduce_sum | solution.py:31
  107.3 0.9 fusion.32
  108.4 3.4 multiply_multiply_fusion.24
  111.8 7.8 %multiply_multiply_fusion.23 = (f32[2,5,256,128]{3,0,2,1:T(2,128)S(1)}, f32[2,5,256,128]{3,0,2,1:T(2,128)S(1)}, f32[2,5,256,128]{3,0,2,1:T(2,128)S(1)}, f32[2,5,...) fusion(f32[2,256,128]{2,0,1:T(2,128)S(1)} %copy.208, ...), kind=kLoop, calls=%fused_computation.20.clone.1 | loop fusion | flops 5898240 | bytes 23200424 | tf_op jit(solution)/shard_map/while/body/eval_jaxpr/transpose(jvp())/mul | solution.py:30
  119.6 16.9 %multiply_reduce_fusion.23 = (f32[2,276,128]{2,0,1:T(2,128)S(1)}, f32[2,276,128]{2,0,1:T(2,128)S(1)}, f32[2,276,128]{2,0,1:T(2,128)S(1)}, f32[2,5,276,128]{3,0,2,1:T(2,128)S(1)}) fusion(f32[2,5]{0,1:T(8,128)S(1)} %copy.165, f32[2,5]{0,1:T(8,128)S(1)} %copy.166, f32[2,5]{0,1:T(8,128)S(1)} %copy.167, f32[2,5,256,128]{3,0,2,1:T(2,128)S(1)} %get-tuple-element.636, ...), kind=kLoop, calls=%fused_computation.40.clone.1 | loop fusion | flops 8973312 | bytes 29786232 | tf_op jit(solution)/shard_map/while/body/eval_jaxpr/transpose(jvp())/reduce_sum | solution.py:27
  136.5 36.5 %multiply_reduce_fusion.24 = (f32[2,276,128]{2,0,1:T(2,128)S(1)}, f32[2,276,128]{2,0,1:T(2,128)S(1)}, f32[2,276,128]{2,0,1:T(2,128)S(1)}, f32[2,276,128]{2,0,1:T...) fusion(f32[2,5,276,128]{3,0,2,1:T(2,128)S(1)} %get-tuple-elemen, ...), kind=kLoop, calls=%fused_computation.41.clone.1 | loop fusion | flops 11446272 | bytes 6501072 | tf_op jit(solution)/shard_map/while/body/eval_jaxpr/transpose(jvp())/reduce_sum | solution.py:27
  173.1 12.5 %add_add_fusion.2 = f32[2,276,148]{2,0,1:T(2,128)S(1)} fusion(f32[2,276,128]{2,0,1:T(2,128)S(1)} %get-tuple-element.658, f32[2,276,128]{2,0,1:T(2,128)S(1)} %get-tuple-element.659, f32[2,276,128]{2,0,1:T(2,128)S(1)} %get-tuple-element.660, f32[2,276,128]{2,0,1:T(2,128)S(1)} %get-tuple-element.661, f32[2,276,128]{2,0,1:T(2,128)S(1)} %get-tuple-element.662, ...), kind=kLoop, calls=%fused_computation.87.clone.1 | loop fusion | flops 1715616 | bytes 6588680 | tf_op jit(solution)/shard_map/while/body/eval_jaxpr/transpose(jvp())/dynamic_update_slice | solution.py:58
  185.6 48.4 %add.858 = f32[2,292,164]{2,0,1:T(2,128)S(1)} dynamic-update-slice(f32[2,292,164]{2,0,1:T(2,128)S(1)} %copy-done.1, f32[2,276,148]{2,0,1:T(2,128)S(1)} %add_add_fusion.2, s32[]{:T(128)} %constant.90.clone.1..sunk, s32[]{:T(128)S(6)} %select_n.22, s32[]{:T(128)S(6)} %select_n.23) | dynamic-update-slice | bytes 653572 | tf_op jit(solution)/shard_map/while/body/eval_jaxpr/add | solution.py:73
  234.1 0.8 copy-done.2
  235.3 0.7 dynamic_slice.103
  235.9 0.6 fusion.30
  243.1 1.6 convert_bitcast_fusion.2
  244.7 1.0 bitcast_convert_fusion.2
  245.7 1.3 constant_dynamic-slice_fusion.30
  247.0 5.1 %constant_dynamic-slice_fusion.31 = (f32[2,276,128]{2,0,1:T(2,128)S(1)}, f32[2,276,128]{2,0,1:T(2,128)S(1)}, f32[2,276,128]{2,0,1:T(2,128)S(1)}, f32[2,276,128]{...) fusion(f32[2,292,164]{2,0,1:T(2,128)S(1)} %get-tuple-element.75, ...), kind=kLoop, calls=%fused_computation.111.clone.1 | loop fusion | bytes 9609288 | tf_op jit(solution)/shard_map/while/body/eval_jaxpr/jvp()/slice | solution.py:25
  252.1 9.6 %multiply_add_fusion.2 = f32[2,5,276,128]{3,0,2,1:T(2,128)S(1)} fusion(f32[2,276,128]{2,0,1:T(2,128)S(1)} %get-tuple-element.575, f32[2,276,128]{2,0,1:T(2,128)S(1)} %get-tuple-element.576, f32[2,5]{0,1:T(8,128)S(1)} %copy.165, f32[2,276,128]{2,0,1:T(2,128)S(1)} %get-tuple-element.577, f32[2,5]{0,1:T(8,128)S(1)} %copy.167, ...), kind=kLoop, calls=%fused_computation.43.clone.1 | loop fusion | flops 14484480 | bytes 7349064 | tf_op jit(solution)/shard_map/while/body/eval_jaxpr/jvp()/add | solution.py:27
  261.7 8.9 %fusion.31 = f32[2,256,128]{2,0,1:T(2,128)S(1)} fusion(f32[2,5,276,128]{3,0,2,1:T(2,128)S(1)} %multiply_add_fusion.2, f32[5,256,128]{2,1,0:T(8,128)S(1)} %bitcast_convert_fusion.2, f32[2,5]{0,1:T(8,128)S(1)} %copy.187, f32[2,5]{0,1:T(8,128)S(1)} %copy.188, f32[2,5]{0,1:T(8,128)S(1)} %copy.189, f32[2,5]{0,1:T(8,128)S(1)} %copy.190, ...), kind=kLoop, calls=%fused_computation.86.clone.1 | loop fusion | flops 14024704 | bytes 28443464 | tf_op jit(solution)/shard_map/while/body/eval_jaxpr/jvp()/reduce_sum | solution.py:31
  270.6 0.9 fusion.32
  271.7 3.4 multiply_multiply_fusion.24
  275.1 7.8 %multiply_multiply_fusion.23 = (f32[2,5,256,128]{3,0,2,1:T(2,128)S(1)}, f32[2,5,256,128]{3,0,2,1:T(2,128)S(1)}, f32[2,5,256,128]{3,0,2,1:T(2,128)S(1)}, f32[2,5,...) fusion(f32[2,256,128]{2,0,1:T(2,128)S(1)} %copy.208, ...), kind=kLoop, calls=%fused_computation.20.clone.1 | loop fusion | flops 5898240 | bytes 23200424 | tf_op jit(solution)/shard_map/while/body/eval_jaxpr/transpose(jvp())/mul | solution.py:30
  282.9 16.9 %multiply_reduce_fusion.23 = (f32[2,276,128]{2,0,1:T(2,128)S(1)}, f32[2,276,128]{2,0,1:T(2,128)S(1)}, f32[2,276,128]{2,0,1:T(2,128)S(1)}, f32[2,5,276,128]{3,0,2,1:T(2,128)S(1)}) fusion(f32[2,5]{0,1:T(8,128)S(1)} %copy.165, f32[2,5]{0,1:T(8,128)S(1)} %copy.166, f32[2,5]{0,1:T(8,128)S(1)} %copy.167, f32[2,5,256,128]{3,0,2,1:T(2,128)S(1)} %get-tuple-element.636, ...), kind=kLoop, calls=%fused_computation.40.clone.1 | loop fusion | flops 8973312 | bytes 29786232 | tf_op jit(solution)/shard_map/while/body/eval_jaxpr/transpose(jvp())/reduce_sum | solution.py:27
  299.8 36.8 %multiply_reduce_fusion.24 = (f32[2,276,128]{2,0,1:T(2,128)S(1)}, f32[2,276,128]{2,0,1:T(2,128)S(1)}, f32[2,276,128]{2,0,1:T(2,128)S(1)}, f32[2,276,128]{2,0,1:T...) fusion(f32[2,5,276,128]{3,0,2,1:T(2,128)S(1)} %get-tuple-elemen, ...), kind=kLoop, calls=%fused_computation.41.clone.1 | loop fusion | flops 11446272 | bytes 6501072 | tf_op jit(solution)/shard_map/while/body/eval_jaxpr/transpose(jvp())/reduce_sum | solution.py:27
  336.6 12.5 %add_add_fusion.2 = f32[2,276,148]{2,0,1:T(2,128)S(1)} fusion(f32[2,276,128]{2,0,1:T(2,128)S(1)} %get-tuple-element.658, f32[2,276,128]{2,0,1:T(2,128)S(1)} %get-tuple-element.659, f32[2,276,128]{2,0,1:T(2,128)S(1)} %get-tuple-element.660, f32[2,276,128]{2,0,1:T(2,128)S(1)} %get-tuple-element.661, f32[2,276,128]{2,0,1:T(2,128)S(1)} %get-tuple-element.662, ...), kind=kLoop, calls=%fused_computation.87.clone.1 | loop fusion | flops 1715616 | bytes 6588680 | tf_op jit(solution)/shard_map/while/body/eval_jaxpr/transpose(jvp())/dynamic_update_slice | solution.py:58
  349.2 48.2 %add.858 = f32[2,292,164]{2,0,1:T(2,128)S(1)} dynamic-update-slice(f32[2,292,164]{2,0,1:T(2,128)S(1)} %copy-done.1, f32[2,276,148]{2,0,1:T(2,128)S(1)} %add_add_fusion.2, s32[]{:T(128)} %constant.90.clone.1..sunk, s32[]{:T(128)S(6)} %select_n.22, s32[]{:T(128)S(6)} %select_n.23) | dynamic-update-slice | bytes 653572 | tf_op jit(solution)/shard_map/while/body/eval_jaxpr/add | solution.py:73
  397.4 0.8 copy-done.2
  399.6 1.1 copy.108
  400.8 3.5 collective-permute-start.2
  404.4 1.3 collective-permute-start.3
  405.7 3.0 collective-permute-done.2
  408.7 3.8 collective-permute-done.3
  412.5 0.9 fusion.23
  413.5 80.2 %reduce-scatter.2.cloned.1.call-done = f32[2,8,128]{2,1,0:T(8,128)} async-done(((f32[2,256,128]{2,1,0:T(8,128)}), f32[2,8,128]{2,1,0:T(8,128)}) %reduce-scatter.2.cloned.1.call-update) | async-done | bytes 8208 | tf_op jit(solution)/shard_map/reduce_scatter | solution.py:84
  (124 shorter events, 9.2 us)
Async XLA Ops:
  6.5 487.1 %reduce-scatter.2.cloned.1.call-start = ((), (), s32[]{:S(2)}) async-start(), calls=%async_computation.1 | async-start | bytes 270336 | tf_op jit(solution)/shard_map/reduce_scatter | solution.py:84
  56.5 14.8 %copy-start.3 = (f32[2,2,5,21]{3,1,2,0:T(2,128)S(1)}, f32[2,2,5,21]{3,1,2,0:T(2,128)}, u32[]{:S(2)}) copy-start(f32[2,2,5,21]{3,1,2,0:T(2,128)} %param.11) | copy-start | bytes 5044
  56.5 14.8 %copy-start.4 = (f32[2,2,5,21]{3,1,2,0:T(2,128)S(1)}, f32[2,2,5,21]{3,1,2,0:T(2,128)}, u32[]{:S(2)}) copy-start(f32[2,2,5,21]{3,1,2,0:T(2,128)} %param.12) | copy-start | bytes 5044
  56.5 14.8 %copy-start.5 = (s32[2,1,2]{2,1,0:T(1,128)S(1)}, s32[2,1,2]{2,1,0:T(1,128)}, u32[]{:S(2)}) copy-start(s32[2,1,2]{2,1,0:T(1,128)} %param.17) | copy-start | bytes 52
  56.5 14.8 %copy-start.6 = (s32[2,1]{0,1:T(1,128)S(1)}, s32[2,1]{0,1:T(1,128)}, u32[]{:S(2)}) copy-start(s32[2,1]{0,1:T(1,128)} %param.16) | copy-start | bytes 28
  56.9 8.7 %collective-permute-start = (f32[2,256,18]{2,0,1:T(2,128)S(1)}, f32[2,256,18]{2,0,1:T(2,128)S(1)}, u32[]{:S(2)}, u32[]{:S(2)}) collective-permute-start(f32[2,256,18]{2,0,1:T(2,128)S(1)} %get-tuple-element.396), channel_id=1, source_target_pairs={{0,32},{32,64},{64,96},{96,128},{128,160},{160,192},{192,224},{1,3... | collective-permute-start | bytes 110600 | tf_op jit(solution)/shard_map/ppermute | solution.py:17
  60.1 9.3 %collective-permute-start.1 = (f32[2,256,18]{2,0,1:T(2,128)S(1)}, f32[2,256,18]{2,0,1:T(2,128)S(1)}, u32[]{:S(2)}, u32[]{:S(2)}) collective-permute-start(f32[2,256,18]{2,0,1:T(2,128)S(1)} %get-tuple-element.397), channel_id=1, source_target_pairs={{32,0},{64,32},{96,64},{128,96},{160,128},{192,160},{224,192},{33,... | collective-permute-start | bytes 110600 | tf_op jit(solution)/shard_map/ppermute | solution.py:18
  136.5 36.6 %copy-start = (f32[2,292,164]{2,0,1:T(2,128)S(1)}, f32[2,292,164]{2,0,1:T(2,128)}, u32[]{:S(2)}) copy-start(f32[2,292,164]{2,0,1:T(2,128)} %get-tuple-element.715) | copy-start | bytes 1149316 | tf_op jit(solution)/shard_map/while
  173.1 12.5 %copy-start.1 = (f32[2,292,164]{2,0,1:T(2,128)S(1)}, f32[2,292,164]{2,0,1:T(2,128)}, u32[]{:S(2)}) copy-start(f32[2,292,164]{2,0,1:T(2,128)} %get-tuple-element.715) | copy-start | bytes 1149316 | tf_op jit(solution)/shard_map/while
  234.0 0.8 copy-start.2
  299.8 36.8 %copy-start = (f32[2,292,164]{2,0,1:T(2,128)S(1)}, f32[2,292,164]{2,0,1:T(2,128)}, u32[]{:S(2)}) copy-start(f32[2,292,164]{2,0,1:T(2,128)} %get-tuple-element.715) | copy-start | bytes 1149316 | tf_op jit(solution)/shard_map/while
  336.6 12.5 %copy-start.1 = (f32[2,292,164]{2,0,1:T(2,128)S(1)}, f32[2,292,164]{2,0,1:T(2,128)}, u32[]{:S(2)}) copy-start(f32[2,292,164]{2,0,1:T(2,128)} %get-tuple-element.715) | copy-start | bytes 1149316 | tf_op jit(solution)/shard_map/while
  397.4 0.8 copy-start.2
  400.8 7.8 %collective-permute-start.2 = (f32[2,256,18]{2,1,0:T(8,128)S(1)}, f32[2,256,18]{2,1,0:T(8,128)S(1)}, u32[]{:S(2)}, u32[]{:S(2)}) collective-permute-start(f32[2,256,18]{2,1,0:T(8,128)S(1)} %get-tuple-element.394), channel_id=1, source_target_pairs={{0,32},{32,64},{64,96},{96,128},{128,160},{160,192},{192,224},{1,3... | collective-permute-start | bytes 110600 | tf_op jit(solution)/shard_map/ppermute | solution.py:17
  404.4 8.1 %collective-permute-start.3 = (f32[2,256,18]{2,1,0:T(8,128)S(1)}, f32[2,256,18]{2,1,0:T(8,128)S(1)}, u32[]{:S(2)}, u32[]{:S(2)}) collective-permute-start(f32[2,256,18]{2,1,0:T(8,128)S(1)} %get-tuple-element.395), channel_id=1, source_target_pairs={{32,0},{64,32},{96,64},{128,96},{160,128},{192,160},{224,192},{33,... | collective-permute-start | bytes 110600 | tf_op jit(solution)/shard_map/ppermute | solution.py:18
Sparse Core Ops, SparseCore 0:
  413.6 79.9 reduce-scatter.1
where the time goes:
time: 504 us; the launch traced here: 501 us
  other arithmetic  201 us (40%)
  local copies, waits for them, and re-layouts  125 us (25%)
  waiting for transfers between devices  95 us (19%)
  blocking collectives  49.3 us (10%)
  between operations  13.7 us (3%)
  starting transfers between devices  9.35 us (2%)
  loops' own time  7.13 us (1%)
    reduce_sum x4, other arithmetic, predict(): horiz[:, :, index, None, None] * window[:, None, :, index:index + width]  107 us
    add x2, local copies, waits for them, and re-layouts, epoch_step(): return (total + grad, None)  96.6 us
    reduce_scatter x1, waiting for transfers between devices, per_device(): return lax.psum_scatter(inner, 'epoch', scatter_dimension=1, tiled=True)  80.2 us
    all_gather x1, blocking collectives, per_device(): whole = lax.all_gather(scene, 'epoch', axis=1, tiled=True)  49.3 us
    dynamic_update_slice x2, other arithmetic, model(): lax.dynamic_slice(field, (jnp.int32(0), start_row, start_col), (bands, ro...  25 us
    mul x4, other arithmetic, predict(): vert[:, :, index, None, None] * across[:, :, index:index + rows, :]  22.3 us
    add x2, other arithmetic, predict(): across + horiz[:, :, index, None, None] * window[:, None, :, index:index...  19.5 us
    reduce_sum x2, other arithmetic, predict(): return jnp.sum(down * maps[None], axis=1)  17.8 us
  transfers between devices with their start and end apart: 5, of which 5 were waited for; matrix products, arithmetic and copies ran while one was open for 0% of the time, Pallas kernels for 0%

commit v1 on v0

v1 whole, which is shorter than its diff:
```python
import functools

import jax
import jax.numpy as jnp
from jax import lax
from jax.experimental import pallas as pl
from jax.experimental.pallas import tpu as pltpu
from jax.sharding import PartitionSpec as P

BANDS, NBASIS, TAPS = 2, 5, 21
LOCAL = 2
ROWS, W, TILES = 256, 128, 8
HALF = 128
REACH = 10
NX, NZ, NC = 4, 4, 2
F32, BF16 = jnp.float32, jnp.bfloat16
MESH = pl.DeviceIdType.MESH


def split2(value):
    hi = value.astype(BF16)
    return hi, (value - hi.astype(F32)).astype(BF16)


def mm(a, b):
    return jnp.dot(a, b, preferred_element_type=F32)


def prepare_taps(taps_in, taps):
    taps[...] = jnp.zeros_like(taps)
    lane = lax.broadcasted_iota(jnp.int32, (NBASIS, W), 1)
    for e in range(LOCAL):
        for b in range(BANDS):
            taps[0, e, b, 0:NBASIS, 0:TAPS] = taps_in[e, b]
            row = taps[0, e, b, 0:NBASIS, :]
            back = jnp.zeros((NBASIS, W), F32)
            for a in range(TAPS):
                back = jnp.where(lane == TAPS - 1 - a, row[:, a : a + 1], back)
            taps[1, e, b, 0:NBASIS, :] = back


def build_bands(lo, hi, offsets, th, tv, hf, hb, vf, vb):
    row = lax.broadcasted_iota(jnp.int32, (W, W), 0)
    lane = lax.broadcasted_iota(jnp.int32, (W, W), 1)
    near = jnp.abs(row - lane) < W // 2

    def circulant(taps, flipped, e, b, k, shift):
        base = jnp.broadcast_to(taps[flipped, e, b, pl.ds(k, 1), :], (8, W))
        for bit in (1, 2, 4):
            base = jnp.where((row[0:8] & bit) != 0, pltpu.roll(base, bit, axis=1), base)
        base = pltpu.roll(base, shift, axis=1)
        full = jnp.concatenate([base] + [pltpu.roll(base, g, axis=1) for g in range(8, W, 8)], axis=0)
        return jnp.where(near, full, 0.0), jnp.where(near, 0.0, full)

    def step(i, carry):
        b, k = i // NBASIS, i % NBASIS
        for e in range(LOCAL):
            dy, dx = offsets[e, 0, 0], offsets[e, 0, 1]
            main, edge = circulant(th, 1, e, b, k, W - REACH - dx)
            for part, (m, s) in enumerate(zip(split2(main), split2(edge))):
                hf[part, b, k, 0:W, e * W : (e + 1) * W] = m
                hf[part, b, k, W : 2 * W, e * W : (e + 1) * W] = s
            main, edge = circulant(th, 0, e, b, k, W - REACH + dx)
            for part, (m, s) in enumerate(zip(split2(main), split2(edge))):
                hb[part, b, e, k, :, 0:W] = m
                hb[part, b, e, k, :, W : 2 * W] = s
            main, edge = circulant(tv, 0, e, b, k, W - REACH + dy)
            for part, (m, s) in enumerate(zip(split2(main), split2(edge))):
                vf[part, b, e, k, :, 0:W] = m
                vf[part, b, e, k, :, W : 2 * W] = s
            main, edge = circulant(tv, 1, e, b, k, W - REACH - dy)
            for part, (m, s) in enumerate(zip(split2(main), split2(edge))):
                vb[part, b, e, k, :, 0:W] = m
                vb[part, b, e, k, :, W : 2 * W] = s
        return carry

    lax.fori_loop(lo, hi, step, 0)


def blocks(top, bottom):
    zero = jnp.zeros((HALF // 2, W), BF16)
    left = jnp.concatenate([top, bottom[0 : HALF // 2], zero], axis=0)
    right = jnp.concatenate([bottom, zero, top[HALF // 2 : HALF]], axis=0)
    return jnp.concatenate([left, right], axis=1)


def side(value):
    return jnp.concatenate([value[0:HALF], value[HALF:ROWS]], axis=1)


def compute_band(b, field, grad, coverage, cv, ov, gv, hf, hb, vf, vb, am, pm):
    main = field[b, 0].reshape(ROWS, W)
    edge = field[b, 1].reshape(ROWS, W)
    x_hi, x_lo = split2(jnp.concatenate([main, edge], axis=1))

    def across(k, carry):
        h_hi, h_lo = hf[0, b, k], hf[1, b, k]
        a = mm(x_hi, h_hi) + mm(x_lo, h_hi) + mm(x_hi, h_lo)
        a_hi, a_lo = split2(a)
        am[0, k] = a_hi
        am[1, k] = a_lo
        return carry

    lax.fori_loop(0, NBASIS, across, 0)

    for e in range(LOCAL):
        cols = slice(e * W, (e + 1) * W)
        model = jnp.zeros((HALF, 2 * W), F32)
        for k in range(NBASIS):
            r_hi = blocks(am[0, k, 0:HALF, cols], am[0, k, HALF:ROWS, cols])
            r_lo = blocks(am[1, k, 0:HALF, cols], am[1, k, HALF:ROWS, cols])
            v_hi, v_lo = vf[0, b, e, k], vf[1, b, e, k]
            down = mm(v_hi, r_hi) + mm(v_hi, r_lo) + mm(v_lo, r_hi)
            model = model + side(cv[e, k]).astype(F32) * down
        weight = (side(gv[e]) * coverage[e, 0]).astype(F32)
        residual = weight * (model - side(ov[e, b]).astype(F32))
        for k in range(NBASIS):
            q_hi, q_lo = split2(side(cv[e, k]).astype(F32) * residual)
            r_hi = blocks(q_hi[:, 0:W], q_hi[:, W : 2 * W])
            r_lo = blocks(q_lo[:, 0:W], q_lo[:, W : 2 * W])
            v_hi, v_lo = vb[0, b, e, k], vb[1, b, e, k]
            up = mm(v_hi, r_hi) + mm(v_hi, r_lo) + mm(v_lo, r_hi)
            for part, p in enumerate(split2(up)):
                at = (e * NBASIS + k) * W
                pm[part, 0:HALF, at : at + W] = p[:, 0:W]
                pm[part, HALF:ROWS, at : at + W] = p[:, W : 2 * W]

    depth = LOCAL * NBASIS * W
    h_hi = hb[0, b].reshape(depth, 2 * W)
    h_lo = hb[1, b].reshape(depth, 2 * W)
    g = mm(pm[0], h_hi) + mm(pm[1], h_hi) + mm(pm[0], h_lo)
    shape = grad.shape[2:]
    grad[b, 0] = g[:, 0:W].reshape(shape)
    grad[b, 1] = g[:, W : 2 * W].reshape(shape)


def kernel(
    scene, kh, kv, coeffs, observed, good, coverage, offsets, out,
    field, left, right, grad, from_core, half, from_x, quarter, from_z, from_left, from_right,
    cv, ov, gv, th, tv, hf, hb, vf, vb, am, pm,
    local_sem, zs, zr, ts, tr, xs, xr, cs, cr, zs2, zr2, ts2, tr2, xs2, xr2, cs2, cr2,
):
    t, me = lax.axis_index("tile"), lax.axis_index("epoch")
    x, z, c = me // (NZ * NC), (me // NC) % NZ, me % NC

    def at(tile, xx, zz, cc):
        return {"tile": tile, "epoch": (xx * NZ + zz) * NC + cc}

    def remote(src, dst, ssem, rsem, where):
        return pltpu.make_async_remote_copy(
            src_ref=src, dst_ref=dst, send_sem=ssem, recv_sem=rsem, device_id=where, device_id_type=MESH
        )

    z_peers = [at(t, x, (z + d) % NZ, c) for d in range(1, NZ)]
    x_peers = [at(t, (x + d) % NX, z, c) for d in range(1, NX)]
    core_peer = at(t, x, z, 1 - c)
    ahead = [at((t + 1) % TILES, x, (z + d) % NZ, c) for d in range(NZ)]
    behind = [at((t + TILES - 1) % TILES, x, (z + d) % NZ, c) for d in range(NZ)]
    everyone = z_peers + x_peers + [core_peer] + ahead + behind

    barrier = pltpu.get_barrier_semaphore()
    for peer in everyone:
        pl.semaphore_signal(barrier, inc=1, device_id=peer, device_id_type=MESH)
    own = pltpu.make_async_copy(scene, field.at[:, 0, x, z, c], local_sem.at[0])
    loads = [
        pltpu.make_async_copy(coeffs, cv, local_sem.at[1]),
        pltpu.make_async_copy(observed, ov, local_sem.at[2]),
        pltpu.make_async_copy(good, gv, local_sem.at[3]),
    ]
    own.start()
    for load in loads:
        load.start()
    own.wait()
    pl.semaphore_wait(barrier, len(everyone))

    mine = field.at[:, 0, x, z, c]
    stage = [remote(mine, mine, zs.at[d], zr.at[d], z_peers[d]) for d in range(NZ - 1)]
    stage += [remote(mine, left.at[:, z], ts.at[d], tr.at[d], ahead[d]) for d in range(NZ)]
    stage += [remote(mine, right.at[:, z], ts.at[NZ + d], tr.at[NZ + d], behind[d]) for d in range(NZ)]
    for copy in stage:
        copy.start()
    prepare_taps(kh, th)
    prepare_taps(kv, tv)
    build_bands(0, 3, offsets, th, tv, hf, hb, vf, vb)
    for copy in stage:
        copy.wait()
    lane = lax.broadcasted_iota(jnp.int32, (BANDS, NZ, 8, W), 3)
    low = jnp.where(t < TILES - 1, right[...], 0.0)
    high = jnp.where(t > 0, left[...], 0.0)
    field[:, 1, x, :, c] = jnp.where(lane < W // 2, low, high)

    mine = field.at[:, :, x, :, c]
    stage = [remote(mine, mine, xs.at[d], xr.at[d], x_peers[d]) for d in range(NX - 1)]
    for copy in stage:
        copy.start()
    build_bands(3, 7, offsets, th, tv, hf, hb, vf, vb)
    for copy in stage:
        copy.wait()

    mine = field.at[:, :, :, :, c]
    copy = remote(mine, mine, cs, cr, core_peer)
    copy.start()
    build_bands(7, BANDS * NBASIS, offsets, th, tv, hf, hb, vf, vb)
    for load in loads:
        load.wait()
    copy.wait()

    def band_step(b, carry):
        compute_band(b, field, grad, coverage, cv, ov, gv, hf, hb, vf, vb, am, pm)
        return carry

    lax.fori_loop(0, BANDS, band_step, 0)

    copy = remote(grad.at[:, :, :, :, 1 - c], from_core, cs2, cr2, core_peer)
    copy.start()
    copy.wait()
    half[...] = grad[:, :, :, :, c] + from_core[...]

    stage = [
        remote(half.at[:, :, (x + d) % NX], from_x.at[d - 1], xs2.at[d - 1], xr2.at[d - 1], x_peers[d - 1])
        for d in range(1, NX)
    ]
    for copy in stage:
        copy.start()
    for copy in stage:
        copy.wait()
    quarter[...] = half[:, :, x] + from_x[0] + from_x[1] + from_x[2]

    stage = [
        remote(quarter.at[:, 0, (z + d) % NZ], from_z.at[d - 1], zs2.at[d - 1], zr2.at[d - 1], z_peers[d - 1])
        for d in range(1, NZ)
    ]
    stage += [
        remote(quarter.at[:, 1, (z + d) % NZ], from_left.at[z], ts2.at[d], tr2.at[d], ahead[d]) for d in range(NZ)
    ]
    stage += [
        remote(quarter.at[:, 1, (z + d) % NZ], from_right.at[z], ts2.at[NZ + d], tr2.at[NZ + d], behind[d])
        for d in range(NZ)
    ]
    for copy in stage:
        copy.start()
    for copy in stage:
        copy.wait()
    lane = lax.broadcasted_iota(jnp.int32, (BANDS, 8, W), 2)
    lower = jnp.where((lane < W // 2) & (t > 0), jnp.sum(from_left[...], axis=0), 0.0)
    upper = jnp.where((lane >= W // 2) & (t < TILES - 1), jnp.sum(from_right[...], axis=0), 0.0)
    out[...] = quarter[:, 0, z] + jnp.sum(from_z[...], axis=0) + lower + upper


def per_device(scene, kernels_h, kernels_v, coeffs, observed, good_pixels, coverage, offsets):
    vmem = pl.BlockSpec(memory_space=pltpu.VMEM)
    smem = pl.BlockSpec(memory_space=pltpu.SMEM)
    hbm = pl.BlockSpec(memory_space=pl.ANY)
    tile = (8, W)
    dma = pltpu.SemaphoreType.DMA
    scratch = [
        pltpu.VMEM((BANDS, 2, NX, NZ, NC) + tile, F32),
        pltpu.VMEM((BANDS, NZ) + tile, F32),
        pltpu.VMEM((BANDS, NZ) + tile, F32),
        pltpu.VMEM((BANDS, 2, NX, NZ, NC) + tile, F32),
        pltpu.VMEM((BANDS, 2, NX, NZ) + tile, F32),
        pltpu.VMEM((BANDS, 2, NX, NZ) + tile, F32),
        pltpu.VMEM((NX - 1, BANDS, 2, NZ) + tile, F32),
        pltpu.VMEM((BANDS, 2, NZ) + tile, F32),
        pltpu.VMEM((NZ - 1, BANDS) + tile, F32),
        pltpu.VMEM((NZ, BANDS) + tile, F32),
        pltpu.VMEM((NZ, BANDS) + tile, F32),
        pltpu.VMEM(coeffs.shape, BF16),
        pltpu.VMEM(observed.shape, BF16),
        pltpu.VMEM(good_pixels.shape, jnp.int32),
        pltpu.VMEM((2, LOCAL, BANDS, 8, W), F32),
        pltpu.VMEM((2, LOCAL, BANDS, 8, W), F32),
        pltpu.VMEM((2, BANDS, NBASIS, 2 * W, LOCAL * W), BF16),
        pltpu.VMEM((2, BANDS, LOCAL, NBASIS, W, 2 * W), BF16),
        pltpu.VMEM((2, BANDS, LOCAL, NBASIS, HALF, 2 * HALF), BF16),
        pltpu.VMEM((2, BANDS, LOCAL, NBASIS, HALF, 2 * HALF), BF16),
        pltpu.VMEM((2, NBASIS, ROWS, LOCAL * W), BF16),
        pltpu.VMEM((2, ROWS, LOCAL * NBASIS * W), BF16),
        dma((4,)),
        dma((NZ - 1,)), dma((NZ - 1,)), dma((2 * NZ,)), dma((2 * NZ,)), dma((NX - 1,)), dma((NX - 1,)), dma, dma,
        dma((NZ - 1,)), dma((NZ - 1,)), dma((2 * NZ,)), dma((2 * NZ,)), dma((NX - 1,)), dma((NX - 1,)), dma, dma,
    ]
    return pl.pallas_call(
        kernel,
        out_shape=jax.ShapeDtypeStruct(scene.shape, F32),
        in_specs=[hbm, vmem, vmem, hbm, hbm, hbm, smem, smem],
        out_specs=vmem,
        scratch_shapes=scratch,
        compiler_params=pltpu.CompilerParams(
            collective_id=0, has_side_effects=True, vmem_limit_bytes=40 * 2**20
        ),
    )(scene, kernels_h, kernels_v, coeffs, observed, good_pixels, coverage, offsets)


def solution(mesh):
    in_specs = (
        P(None, "epoch", "tile"),
        P("epoch", None, None, None),
        P("epoch", None, None, None),
        P("epoch", None, None, "tile"),
        P("epoch", None, None, "tile"),
        P("epoch", None, "tile"),
        P("epoch", "tile"),
        P("epoch", "tile", None),
    )
    out_specs = P(None, "epoch", "tile")
    return jax.shard_map(
        per_device, mesh=mesh, in_specs=in_specs, out_specs=out_specs, check_vma=False
    )
```

time: 504 us -> 49.7 us (0.10)
  other arithmetic: 201 us -> 0 us
  local copies, waits for them, and re-layouts: 125 us -> 5.74 us
  waiting for transfers between devices: 95 us -> 0 us
  blocking collectives: 49.3 us -> 0 us
  Pallas kernels: 0 us -> 43.7 us
  between operations: 13.7 us -> 0.03 us
  starting transfers between devices: 9.35 us -> 0 us
  loops' own time: 7.13 us -> 0 us
    reduce_sum x6 -> x0, other arithmetic: 125 us -> none  [the longest x4 107 us: predict(): horiz[:, :, index, None, None] * window[:, None, :, index:index + width]]
    add x2 -> x0, local copies, waits for them, and re-layouts: 96.6 us -> none  [epoch_step(): return (total + grad, None)]
    reduce_scatter x1 -> x0, waiting for transfers between devices: 80.2 us -> none  [per_device(): return lax.psum_scatter(inner, 'epoch', scatter_dimension=1, tiled=True)]
    all_gather x1 -> x0, blocking collectives: 49.3 us -> none  [per_device(): whole = lax.all_gather(scene, 'epoch', axis=1, tiled=True)]
    pallas_call x0 -> x1, Pallas kernels: none -> 43.7 us  [per_device(): pl.pallas_call(kernel, out_shape=jax.ShapeDtypeStruct(scene.shape, F32),...]
    mul x10 -> x0, other arithmetic: 29.4 us -> none  [the longest x4 22.3 us: predict(): vert[:, :, index, None, None] * across[:, :, index:index + rows, :]]
    dynamic_update_slice x2 -> x0, other arithmetic: 25 us -> none  [model(): lax.dynamic_slice(field, (jnp.int32(0), start_row, start_col), (bands, ro...]
    add x3 -> x0, other arithmetic: 20.4 us -> none  [the longest x2 19.5 us: predict(): across + horiz[:, :, index, None, None] * window[:, None, :, index:index...]
  transfers between devices with their start and end apart: 5 -> 0, of which waited for: 5 -> 0; matrix products, arithmetic and copies ran while one was open for 0% -> 0% of each run, Pallas kernels for 0% -> 0%
where the time goes in v1:
time: 49.7 us; the launch traced here: 49.4 us
  Pallas kernels  43.7 us (88%)
  local copies, waits for them, and re-layouts  5.74 us (12%)
    pallas_call x1, Pallas kernels, per_device(): pl.pallas_call(kernel, out_shape=jax.ShapeDtypeStruct(scene.shape, F32),...  43.7 us
    unnamed x16, local copies, waits for them, and re-layouts  5.74 us

profile of v1, /device:TPU:1, one launch (start us, length us, event | category | flops | bytes accessed | tf_op | source)
XLA Modules:
  0.0 49.4 jit_solution(4301196411964852780)
XLA Ops:
  0.0 0.7 %copy.11.coverage = s32[2,1]{1,0:T(2,128)S(1)} copy(s32[2,1]{0,1:T(1,128)} %param.14) | data formatting | bytes 16 | tf_op args[6]
  0.7 0.0 copy-start.5
  0.7 0.7 %copy.9.kh = f32[2,2,5,21]{3,2,1,0:T(8,128)S(1)} copy(f32[2,2,5,21]{3,1,2,0:T(2,128)} %param.9) | data formatting | bytes 3360 | tf_op args[1]
  1.5 0.0 copy-done.5
  1.5 0.0 copy-start.3
  1.5 0.0 copy-start.4
  1.5 0.7 %copy-done.3 = f32[2,8,128]{2,1,0:T(8,128)S(1)} copy-done((f32[2,8,128]{2,1,0:T(8,128)S(1)}, f32[2,8,128]{2,1,0:T(8,128)}, u32[]{:S(2)}) %copy-start.3) | copy-done | bytes 8216
  2.2 0.0 copy-done.4
  2.2 0.0 copy-start
  2.2 1.1 %copy-done = bf16[2,5,256,128]{3,2,1,0:T(8,128)(2,1)S(1)} copy-done((bf16[2,5,256,128]{3,2,1,0:T(8,128)(2,1)S(1)}, bf16[2,5,256,128]{3,2,1,0:T(8,128)(2,1)}, u32[]{:S(2)}) %copy-start) | copy-done | bytes 655384
  3.3 0.0 copy-start.1
  3.3 0.9 %copy-done.1 = bf16[2,2,256,128]{3,2,1,0:T(8,128)(2,1)S(1)} copy-done((bf16[2,2,256,128]{3,2,1,0:T(8,128)(2,1)S(1)}, bf16[2,2,256,128]{3,2,1,0:T(8,128)(2,1)}, u32[]{:S(2)}) %copy-start.1) | copy-done | bytes 262168
  4.2 0.0 copy-start.2
  4.2 0.9 %copy-done.2 = s32[2,256,128]{2,1,0:T(8,128)S(1)} copy-done((s32[2,256,128]{2,1,0:T(8,128)S(1)}, s32[2,256,128]{2,1,0:T(8,128)}, u32[]{:S(2)}) %copy-start.2) | copy-done | bytes 262168
  5.2 43.7 %shard_map.82 = f32[2,8,128]{2,1,0:T(8,128)S(1)} custom-call(f32[2,8,128]{2,1,0:T(8,128)S(1)} %copy-done.3, f32[2,2,5,21]{3,2,1,0:T(8,128)S(1)} %copy.9.kh, f32[2,2,5,21]{3,2,1,0:T(8,128)S(1)} %copy.10.kv, bf16[2,5,256,128]{3,2,1,0:T(8,128)(2,1)S(1)} %copy-done, bf16[2,2,256,128]{3,2,1,0:T(8,128)(2,1)S(1)} %copy-done.1, s32[2,256,128]{2,1,0:T(8,128)S(1)} %copy-done.2, ...), custom_call_target="tpu_custom_call" | custom-call | tf_op jit(solution)/shard_map/pallas_call | solution.py:283
  48.8 0.6 %copy.13 = f32[2,8,128]{2,1,0:T(8,128)} copy(f32[2,8,128]{2,1,0:T(8,128)S(1)} %shard_map.82) | data formatting | bytes 16384
  (1 shorter events, 0.0 us)
Async XLA Ops:
  0.7 0.7 %copy-start.5 = (f32[2,2,5,21]{3,1,2,0:T(2,128)S(1)}, f32[2,2,5,21]{3,1,2,0:T(2,128)}, u32[]{:S(2)}) copy-start(f32[2,2,5,21]{3,1,2,0:T(2,128)} %param.10) | copy-start | bytes 5044
  1.5 0.7 %copy-start.3 = (f32[2,8,128]{2,1,0:T(8,128)S(1)}, f32[2,8,128]{2,1,0:T(8,128)}, u32[]{:S(2)}) copy-start(f32[2,8,128]{2,1,0:T(8,128)} %scene.1) | copy-start | bytes 24580
  1.5 0.7 %copy-start.4 = (s32[2,1,2]{2,1,0:T(1,128)S(1)}, s32[2,1,2]{2,1,0:T(1,128)}, u32[]{:S(2)}) copy-start(s32[2,1,2]{2,1,0:T(1,128)} %offsets.1) | copy-start | bytes 52
  2.2 1.1 %copy-start = (bf16[2,5,256,128]{3,2,1,0:T(8,128)(2,1)S(1)}, bf16[2,5,256,128]{3,2,1,0:T(8,128)(2,1)}, u32[]{:S(2)}) copy-start(bf16[2,5,256,128]{3,2,1,0:T(8,128)(2,1)} %coeffs.1) | copy-start | bytes 1966084
  3.3 0.9 %copy-start.1 = (bf16[2,2,256,128]{3,2,1,0:T(8,128)(2,1)S(1)}, bf16[2,2,256,128]{3,2,1,0:T(8,128)(2,1)}, u32[]{:S(2)}) copy-start(bf16[2,2,256,128]{3,2,1,0:T(8,128)(2,1)} %observed.1) | copy-start | bytes 786436
  4.2 0.9 %copy-start.2 = (s32[2,256,128]{2,1,0:T(8,128)S(1)}, s32[2,256,128]{2,1,0:T(8,128)}, u32[]{:S(2)}) copy-start(s32[2,256,128]{2,1,0:T(8,128)} %good.1) | copy-start | bytes 786436

commit v2 on v0

v2 whole, which is shorter than its diff:
```python
import jax
import jax.numpy as jnp
from jax import lax
from jax.experimental import pallas as pl
from jax.experimental.pallas import tpu as pltpu
from jax.sharding import PartitionSpec as P

BANDS, NBASIS, TAPS = 2, 5, 21
LOCAL = 2
ROWS, W, TILES = 256, 128, 8
HALF = 128
REACH = 10
NX, NZ, NC = 4, 4, 2
F32, BF16 = jnp.float32, jnp.bfloat16
MESH = pl.DeviceIdType.MESH


def split2(value):
    hi = value.astype(BF16)
    return hi, (value - hi.astype(F32)).astype(BF16)


def mm(a, b):
    return jnp.dot(a, b, preferred_element_type=F32)


def prepare_taps(taps_in, taps):
    taps[...] = jnp.zeros_like(taps)
    lane = lax.broadcasted_iota(jnp.int32, (8, W), 1)
    for e in range(LOCAL):
        for b in range(BANDS):
            taps[0, e, b, 0:NBASIS, 0:TAPS] = taps_in[e, :, b, :]

    def step(i, carry):
        row = taps[0, i // BANDS, i % BANDS]
        back = jnp.zeros((8, W), F32)
        for a in range(TAPS):
            back = jnp.where(lane == TAPS - 1 - a, row[:, a : a + 1], back)
        taps[1, i // BANDS, i % BANDS] = back
        return carry

    lax.fori_loop(0, LOCAL * BANDS, step, 0)


def build_bands(offsets, th, tv, hf, hb, vf, vb):
    row = lax.broadcasted_iota(jnp.int32, (W, W), 0)
    lane = lax.broadcasted_iota(jnp.int32, (W, W), 1)
    near = jnp.abs(row - lane) < W // 2

    def circulant(taps, flipped, e, b, k, shift):
        base = jnp.broadcast_to(taps[flipped, e, b, pl.ds(k, 1), :], (8, W))
        for bit in (1, 2, 4):
            base = jnp.where((row[0:8] & bit) != 0, pltpu.roll(base, bit, axis=1), base)
        base = pltpu.roll(base, shift, axis=1)
        full = jnp.concatenate([base] + [pltpu.roll(base, g, axis=1) for g in range(8, W, 8)], axis=0)
        return split2(jnp.where(near, full, 0.0)), split2(jnp.where(near, 0.0, full))

    def step(i, carry):
        b, k = i // NBASIS, i % NBASIS
        first = pl.ds(pl.multiple_of(b * (W // 2), W // 2), W // 2)
        second = pl.ds(pl.multiple_of((1 - b) * (W // 2), W // 2), W // 2)
        for e in range(LOCAL):
            dy, dx = offsets[e, 0, 0], offsets[e, 0, 1]
            cols = slice(e * W, (e + 1) * W)
            main, edge = circulant(th, 1, e, b, k, W - REACH - dx)
            for part in range(2):
                hf[part, b, k, 0, :, cols] = main[part]
                hf[part, b, k, 1, first, cols] = edge[part][0 : W // 2]
                hf[part, b, k, 1, second, cols] = edge[part][W // 2 : W]
            main, edge = circulant(th, 0, e, b, k, W - REACH + dx)
            for part in range(2):
                hb[part, b, e, k, :, 0:W] = main[part]
                hb[part, b, e, k, :, W : 2 * W] = edge[part]
            main, edge = circulant(tv, 0, e, b, k, W - REACH + dy)
            for part in range(2):
                vf[part, b, e, k, :, 0:W] = main[part]
                vf[part, b, e, k, :, W : 2 * W] = edge[part]
            main, edge = circulant(tv, 1, e, b, k, W - REACH - dy)
            for part in range(2):
                vb[part, b, e, k, :, 0:W] = main[part]
                vb[part, b, e, k, :, W : 2 * W] = edge[part]
        return carry

    lax.fori_loop(0, BANDS * NBASIS, step, 0)


def blocks(top, bottom):
    zero = jnp.zeros((HALF // 2, W), BF16)
    left = jnp.concatenate([top, bottom[0 : HALF // 2], zero], axis=0)
    right = jnp.concatenate([bottom, zero, top[HALF // 2 : HALF]], axis=0)
    return jnp.concatenate([left, right], axis=1)


def side(value):
    return jnp.concatenate([value[0:HALF], value[HALF:ROWS]], axis=1)


def mm3(a, b):
    if a[0].shape[1] < 2 * W:
        wide = mm(jnp.concatenate(a, axis=1), jnp.concatenate([b[0], b[0]], axis=0))
        return wide + mm(a[0], b[1])
    return mm(a[0], b[0]) + mm(a[1], b[0]) + mm(a[0], b[1])


def both(ref, *index):
    return ref[(0,) + index], ref[(1,) + index]


def epoch_terms(b, e, coverage, cv, ov, gv, vf, vb, am, pm):
    model = jnp.zeros((HALF, 2 * W), F32)
    for k in range(NBASIS):
        rows = [blocks(am[part, b, e, k, 0:HALF], am[part, b, e, k, HALF:ROWS]) for part in range(2)]
        model = model + side(cv[e, k]).astype(F32) * mm3(both(vf, b, e, k), rows)
    weight = (side(gv[e]) * coverage[0, e]).astype(F32)
    residual = weight * (model - side(ov[e, b]).astype(F32))
    for k in range(NBASIS):
        q = split2(side(cv[e, k]).astype(F32) * residual)
        rows = [blocks(part[:, 0:W], part[:, W : 2 * W]) for part in q]
        up = mm3(both(vb, b, e, k), rows)
        for part, p in enumerate(split2(up)):
            pm[part, e * NBASIS + k, 0:HALF] = p[:, 0:W]
            pm[part, e * NBASIS + k, HALF:ROWS] = p[:, W : 2 * W]


def kernel(
    scene, kh, kv, coeffs, observed, good, coverage_in, offsets_in, out,
    field, packed, sides, left, right, grad, from_core, half, from_e, from_left, from_right,
    khv, kvv, cv, ov, gv, coverage, offsets, th, tv, hf, hb, vf, vb, af, am, pm,
    local_sem, es, er, ss, sr, cs, cr, es2, er2, ss2, sr2, cs2, cr2,
):
    t, me = lax.axis_index("tile"), lax.axis_index("epoch")
    x, z, c = me // (NZ * NC), (me // NC) % NZ, me % NC

    def at(tile, xx, zz, cc):
        return {"tile": tile, "epoch": (xx * NZ + zz) * NC + cc}

    def remote(src, dst, ssem, rsem, where):
        return pltpu.make_async_remote_copy(
            src_ref=src, dst_ref=dst, send_sem=ssem, recv_sem=rsem, device_id=where, device_id_type=MESH
        )

    def signal(where):
        pl.semaphore_signal(barrier, inc=1, device_id=where, device_id_type=MESH)

    spots = [((x + i) % NX, (z + j) % NZ) for i in range(NX) for j in range(NZ)]
    spots = spots[1:] + spots[:1]
    near = NX * NZ - 1
    has_left, has_right = t > 0, t < TILES - 1

    barrier = pltpu.get_barrier_semaphore()
    own = pltpu.make_async_copy(scene, field.at[:, x, z, c], local_sem.at[0])
    own.start()
    @pl.when(has_right)
    def _():
        for xx, zz in spots:
            signal(at(t + 1, xx, zz, c))

    @pl.when(has_left)
    def _():
        for xx, zz in spots:
            signal(at(t - 1, xx, zz, c))

    for xx, zz in spots[:near]:
        signal(at(t, xx, zz, c))
    signal(at(t, x, z, 1 - c))

    small = [
        pltpu.make_async_copy(kh, khv, local_sem.at[1]),
        pltpu.make_async_copy(kv, kvv, local_sem.at[2]),
        pltpu.make_async_copy(coverage_in, coverage, local_sem.at[3]),
        pltpu.make_async_copy(offsets_in, offsets, local_sem.at[4]),
    ]
    loads = [
        pltpu.make_async_copy(coeffs, cv, local_sem.at[5]),
        pltpu.make_async_copy(observed, ov, local_sem.at[6]),
        pltpu.make_async_copy(good, gv, local_sem.at[7]),
    ]
    for load in small + loads:
        load.start()
    own.wait()
    lane = lax.broadcasted_iota(jnp.int32, (8, W), 1)
    outer = (lane < W // 4) | (lane >= 3 * W // 4)
    turned = pltpu.roll(field[1, x, z, c], W // 2, axis=1)
    packed[...] = jnp.where(outer, field[0, x, z, c], turned)
    count = near + 1 + len(spots) * (has_left.astype(jnp.int32) + has_right.astype(jnp.int32))
    pl.semaphore_wait(barrier, count)

    mine = field.at[:, x, z, c]
    mains = [remote(mine, mine, es.at[d], er.at[d], at(t, *spots[d], c)) for d in range(near)]
    n = len(spots)
    slot = x * NZ + z
    to_right = [remote(packed, left.at[slot], ss.at[d], sr.at[d], at(t + 1, *spots[d], c)) for d in range(n)]
    to_left = [remote(packed, right.at[slot], ss.at[n + d], sr.at[n + d], at(t - 1, *spots[d], c)) for d in range(n)]
    @pl.when(has_right)
    def _():
        for copy in to_right:
            copy.start()

    @pl.when(has_left)
    def _():
        for copy in to_left:
            copy.start()

    for copy in mains:
        copy.start()

    for load in small:
        load.wait()
    prepare_taps(khv, th)
    prepare_taps(kvv, tv)
    build_bands(offsets, th, tv, hf, hb, vf, vb)
    for copy in mains:
        copy.wait_recv()
    rows = field.at[:, :, :, c]
    swap = remote(rows, rows, cs.at[0], cr.at[0], at(t, x, z, 1 - c))
    swap.start()
    for load in loads:
        load.wait()

    @pl.when(has_left)
    def _():
        for copy in to_right:
            copy.wait_recv()

    @pl.when(has_right)
    def _():
        for copy in to_left:
            copy.wait_recv()

    lane = lax.broadcasted_iota(jnp.int32, (n, 8, W), 2)
    from_right_side = (lane // (W // 4)) % 2 == 0
    low = jnp.where(has_right, right[...], 0.0)
    high = jnp.where(has_left, left[...], 0.0)
    sides[:, :, c] = jnp.where(from_right_side, low, high).reshape(NX, NZ, 8, W)
    rows = sides.at[:, :, c]
    swap_sides = remote(rows, rows, cs.at[1], cr.at[1], at(t, x, z, 1 - c))
    swap_sides.start()

    swap.wait_recv()
    parts = [split2(field[b].reshape(ROWS, W)) for b in range(BANDS)]

    def own_columns(k, carry):
        for b in range(BANDS):
            af[b, k] = mm3(parts[b], both(hf, b, k, 0))
        return carry

    lax.fori_loop(0, NBASIS, own_columns, 0)
    swap_sides.wait_recv()
    beside = split2(sides[...].reshape(ROWS, W))

    def side_columns(k, carry):
        for b in range(BANDS):
            a = split2(af[b, k] + mm3(beside, both(hf, b, k, 1)))
            for part in range(2):
                for e in range(LOCAL):
                    am[part, b, e, k] = a[part][:, e * W : (e + 1) * W]
        return carry

    lax.fori_loop(0, NBASIS, side_columns, 0)

    depth = LOCAL * NBASIS * W
    shape = grad.shape[1:]

    def across(b, lo):
        h = [hb[part, b, :, :, :, lo : lo + W].reshape(depth, W) for part in range(2)]
        p = [jnp.concatenate([pm[part, i] for i in range(LOCAL * NBASIS)], axis=1) for part in range(2)]
        return mm3(p, h)

    def sum_copy(b):
        return remote(grad.at[b, :, :, 1 - c], from_core.at[b], cs2.at[b], cr2.at[b], at(t, x, z, 1 - c))

    def take_sum(b):
        sum_copy(b).wait_recv()
        half[b] = grad[b, :, :, c] + from_core[b]

    def mains_of(b):
        return [
            remote(half.at[b, spots[d][0], spots[d][1]], from_e.at[b, d], es2.at[b, d], er2.at[b, d], at(t, *spots[d], c))
            for d in range(near)
        ]

    mains0, mains1 = mains_of(0), mains_of(1)
    wide = lax.broadcasted_iota(jnp.int32, (ROWS, W), 1)
    wide = (wide < W // 4) | (wide >= 3 * W // 4)

    def band_step(b, carry):
        def epoch_step(e, carry):
            epoch_terms(b, e, coverage, cv, ov, gv, vf, vb, am, pm)

            @pl.when((b == 1) & (e == 1))
            def _():
                take_sum(0)
                for copy in mains0:
                    copy.start()

            return carry

        lax.fori_loop(0, LOCAL, epoch_step, 0)
        edge = across(b, W)

        @pl.when(b == 0)
        def _():
            grad[BANDS] = edge.reshape(shape)

        @pl.when(b == 1)
        def _():
            first = grad[BANDS].reshape(ROWS, W)
            grad[BANDS] = jnp.where(wide, first, pltpu.roll(edge, W // 2, axis=1)).reshape(shape)
            sum_copy(BANDS).start()

        grad[b] = across(b, 0).reshape(shape)
        sum_copy(b).start()
        return carry

    lax.fori_loop(0, BANDS, band_step, 0)
    take_sum(BANDS)
    to_right2 = [
        remote(half.at[2, spots[d][0], spots[d][1]], from_left.at[slot], ss2.at[d], sr2.at[d], at(t + 1, *spots[d], c))
        for d in range(n)
    ]
    to_left2 = [
        remote(
            half.at[2, spots[d][0], spots[d][1]], from_right.at[slot], ss2.at[n + d], sr2.at[n + d], at(t - 1, *spots[d], c)
        )
        for d in range(n)
    ]

    @pl.when(has_right)
    def _():
        for copy in to_right2:
            copy.start()

    @pl.when(has_left)
    def _():
        for copy in to_left2:
            copy.start()

    take_sum(1)
    for copy in mains1:
        copy.start()

    for copy in mains + [swap, swap_sides] + [sum_copy(b) for b in range(BANDS + 1)] + mains0 + mains1:
        copy.wait_send()

    @pl.when(has_right)
    def _():
        for copy in to_right + to_right2:
            copy.wait_send()

    @pl.when(has_left)
    def _():
        for copy in to_left + to_left2:
            copy.wait_send()

    for copy in mains0 + mains1:
        copy.wait_recv()

    @pl.when(has_left)
    def _():
        for copy in to_right2:
            copy.wait_recv()

    @pl.when(has_right)
    def _():
        for copy in to_left2:
            copy.wait_recv()

    lane = lax.broadcasted_iota(jnp.int32, (8, W), 1)
    lower = jnp.where(has_left, jnp.sum(from_left[...], axis=0), 0.0)
    upper = jnp.where(has_right, jnp.sum(from_right[...], axis=0), 0.0)
    beside = jnp.where((lane // (W // 4)) % 2 == 0, lower, upper)
    for b in range(BANDS):
        add = beside if b == 0 else pltpu.roll(beside, W // 2, axis=1)
        out[b] = half[b, x, z] + jnp.sum(from_e[b], axis=0) + jnp.where(outer, add, 0.0)


def per_device(scene, kernels_h, kernels_v, coeffs, observed, good_pixels, coverage, offsets):
    vmem = pl.BlockSpec(memory_space=pltpu.VMEM)
    hbm = pl.BlockSpec(memory_space=pl.ANY)
    tile = (8, W)
    dma = pltpu.SemaphoreType.DMA
    chips = (NX, NZ)
    n = NX * NZ
    scratch = [
        pltpu.VMEM((BANDS, *chips, NC) + tile, F32),
        pltpu.VMEM(tile, F32),
        pltpu.VMEM((*chips, NC) + tile, F32),
        pltpu.VMEM((n,) + tile, F32),
        pltpu.VMEM((n,) + tile, F32),
        pltpu.VMEM((BANDS + 1, *chips, NC) + tile, F32),
        pltpu.VMEM((BANDS + 1, *chips) + tile, F32),
        pltpu.VMEM((BANDS + 1, *chips) + tile, F32),
        pltpu.VMEM((BANDS, n - 1) + tile, F32),
        pltpu.VMEM((n,) + tile, F32),
        pltpu.VMEM((n,) + tile, F32),
        pltpu.VMEM((LOCAL, NBASIS, BANDS, TAPS), F32),
        pltpu.VMEM((LOCAL, NBASIS, BANDS, TAPS), F32),
        pltpu.VMEM(coeffs.shape, BF16),
        pltpu.VMEM(observed.shape, BF16),
        pltpu.VMEM(good_pixels.shape, jnp.int32),
        pltpu.SMEM((1, LOCAL), jnp.int32),
        pltpu.SMEM(offsets.shape, jnp.int32),
        pltpu.VMEM((2, LOCAL, BANDS, 8, W), F32),
        pltpu.VMEM((2, LOCAL, BANDS, 8, W), F32),
        pltpu.VMEM((2, BANDS, NBASIS, 2, W, LOCAL * W), BF16),
        pltpu.VMEM((2, BANDS, LOCAL, NBASIS, W, 2 * W), BF16),
        pltpu.VMEM((2, BANDS, LOCAL, NBASIS, HALF, 2 * HALF), BF16),
        pltpu.VMEM((2, BANDS, LOCAL, NBASIS, HALF, 2 * HALF), BF16),
        pltpu.VMEM((BANDS, NBASIS, ROWS, LOCAL * W), F32),
        pltpu.VMEM((2, BANDS, LOCAL, NBASIS, ROWS, W), BF16),
        pltpu.VMEM((2, LOCAL * NBASIS, ROWS, W), BF16),
        dma((8,)),
        dma((n - 1,)), dma((n - 1,)), dma((2 * n,)), dma((2 * n,)), dma((2,)), dma((2,)),
        dma((BANDS, n - 1)), dma((BANDS, n - 1)), dma((2 * n,)), dma((2 * n,)), dma((BANDS + 1,)), dma((BANDS + 1,)),
    ]
    return pl.pallas_call(
        kernel,
        out_shape=jax.ShapeDtypeStruct(scene.shape, F32),
        in_specs=[hbm] * 8,
        out_specs=vmem,
        scratch_shapes=scratch,
        compiler_params=pltpu.CompilerParams(
            collective_id=0, has_side_effects=True, vmem_limit_bytes=60 * 2**20
        ),
    )(
        scene,
        kernels_h.transpose(0, 2, 1, 3),
        kernels_v.transpose(0, 2, 1, 3),
        coeffs,
        observed,
        good_pixels,
        coverage.transpose(1, 0),
        offsets,
    )


def solution(mesh):
    in_specs = (
        P(None, "epoch", "tile"),
        P("epoch", None, None, None),
        P("epoch", None, None, None),
        P("epoch", None, None, "tile"),
        P("epoch", None, None, "tile"),
        P("epoch", None, "tile"),
        P("epoch", "tile"),
        P("epoch", "tile", None),
    )
    out_specs = P(None, "epoch", "tile")
    return jax.shard_map(
        per_device, mesh=mesh, in_specs=in_specs, out_specs=out_specs, check_vma=False
    )
```

time: 504 us -> 44.9 us (0.09)
  other arithmetic: 201 us -> 0 us
  local copies, waits for them, and re-layouts: 125 us -> 1.3 us
  waiting for transfers between devices: 95 us -> 0 us
  blocking collectives: 49.3 us -> 0 us
  Pallas kernels: 0 us -> 43.4 us
  between operations: 13.7 us -> 0.01 us
  starting transfers between devices: 9.35 us -> 0 us
  loops' own time: 7.13 us -> 0 us
    reduce_sum x6 -> x0, other arithmetic: 125 us -> none  [the longest x4 107 us: predict(): horiz[:, :, index, None, None] * window[:, None, :, index:index + width]]
    add x2 -> x0, local copies, waits for them, and re-layouts: 96.6 us -> none  [epoch_step(): return (total + grad, None)]
    reduce_scatter x1 -> x0, waiting for transfers between devices: 80.2 us -> none  [per_device(): return lax.psum_scatter(inner, 'epoch', scatter_dimension=1, tiled=True)]
    all_gather x1 -> x0, blocking collectives: 49.3 us -> none  [per_device(): whole = lax.all_gather(scene, 'epoch', axis=1, tiled=True)]
    pallas_call x0 -> x1, Pallas kernels: none -> 43.4 us  [per_device(): pl.pallas_call(kernel, out_shape=jax.ShapeDtypeStruct(scene.shape, F32),...]
    mul x10 -> x0, other arithmetic: 29.4 us -> none  [the longest x4 22.3 us: predict(): vert[:, :, index, None, None] * across[:, :, index:index + rows, :]]
    dynamic_update_slice x2 -> x0, other arithmetic: 25 us -> none  [model(): lax.dynamic_slice(field, (jnp.int32(0), start_row, start_col), (bands, ro...]
    add x3 -> x0, other arithmetic: 20.4 us -> none  [the longest x2 19.5 us: predict(): across + horiz[:, :, index, None, None] * window[:, None, :, index:index...]
  transfers between devices with their start and end apart: 5 -> 0, of which waited for: 5 -> 0; matrix products, arithmetic and copies ran while one was open for 0% -> 0% of each run, Pallas kernels for 0% -> 0%
where the time goes in v2:
time: 44.9 us; the launch traced here: 44.8 us
  Pallas kernels  43.4 us (97%)
  local copies, waits for them, and re-layouts  1.3 us (3%)
    pallas_call x1, Pallas kernels, per_device(): pl.pallas_call(kernel, out_shape=jax.ShapeDtypeStruct(scene.shape, F32),...  43.4 us
    unnamed x1, local copies, waits for them, and re-layouts  1.3 us

profile of v2, /device:TPU:1, one launch (start us, length us, event | category | flops | bytes accessed | tf_op | source)
XLA Modules:
  0.0 44.8 jit_solution(11098209757771667887)
XLA Ops:
  0.0 43.4 %shard_map.82 = f32[2,8,128]{2,1,0:T(8,128)} custom-call(f32[2,8,128]{2,1,0:T(8,128)} %scene.1, f32[2,5,2,21]{3,2,1,0:T(2,128)} %bitcast.3, f32[2,5,2,21]{3,2,1,0:T(2,128)} %bitcast.4, bf16[2,5,256,128]{3,2,1,0:T(8,128)(2,1)} %coeffs.1, bf16[2,2,256,128]{3,2,1,0:T(8,128)(2,1)} %observed.1, s32[2,256,128]{2,1,0:T(8,128)} %good.1, s32[1,2]{1,0:T(1,128)} %bitcast.5, ...), custom_call_target="tpu_custom_call" | custom-call | tf_op jit(solution)/shard_map/pallas_call | solution.py:416
  43.5 1.3 %copy.10 = f32[2,8,128]{2,1,0:T(8,128)} copy(f32[2,8,128]{2,1,0:T(8,128)} %shard_map.82) | data formatting | bytes 16384

commit v3 on v2

--- a/solution.py
+++ b/solution.py
@@ -99,7 +99,11 @@
     if a[0].shape[1] < 2 * W:
         wide = mm(jnp.concatenate(a, axis=1), jnp.concatenate([b[0], b[0]], axis=0))
         return wide + mm(a[0], b[1])
-    return mm(a[0], b[0]) + mm(a[1], b[0]) + mm(a[0], b[1])
+    if a[0].shape[1] > 2 * W:
+        return mm(a[0], b[0]) + mm(a[1], b[0]) + mm(a[0], b[1])
+    rows = a[0].shape[0]
+    tall = mm(jnp.concatenate(a, axis=0), b[0])
+    return tall[0:rows] + tall[rows:] + mm(a[0], b[1])
 
 
 def both(ref, *index):
@@ -122,10 +126,26 @@
             pm[part, e * NBASIS + k, HALF:ROWS] = p[:, W : 2 * W]
 
 
+def right_lanes(shape):
+    return (lax.broadcasted_iota(jnp.int32, shape, len(shape) - 1) // (W // 4)) % 2 == 0
+
+
+def fold(value, to_right):
+    axis = value.ndim - 1
+    below = pltpu.roll(value, 4, axis=axis - 1)
+    below = pltpu.roll(below, W // 4 if to_right else 3 * W // 4, axis=axis)
+    mixed = jnp.where(right_lanes(value.shape) == to_right, value, below)
+    return mixed[..., 0:4, :]
+
+
+def unfold(value, to_right):
+    return pltpu.roll(value, 3 * W // 4 if to_right else W // 4, axis=value.ndim - 1)
+
+
 def kernel(
     scene, kh, kv, coeffs, observed, good, coverage_in, offsets_in, out,
-    field, packed, sides, left, right, grad, from_core, half, from_e, from_left, from_right,
-    khv, kvv, cv, ov, gv, coverage, offsets, th, tv, hf, hb, vf, vb, af, am, pm,
+    field, packed_right, packed_left, sides, left, right, grad, from_core, half, from_e, half_right, half_left, from_left, from_right,
+    khv, kvv, cv, ov, gv, coverage, offsets, th, tv, hf, hb, vf, vb, af, am, pm, beside,
     local_sem, es, er, ss, sr, cs, cr, es2, er2, ss2, sr2, cs2, cr2,
 ):
     t, me = lax.axis_index("tile"), lax.axis_index("epoch")
@@ -142,8 +162,7 @@
     def signal(where):
         pl.semaphore_signal(barrier, inc=1, device_id=where, device_id_type=MESH)
 
-    spots = [((x + i) % NX, (z + j) % NZ) for i in range(NX) for j in range(NZ)]
-    spots = spots[1:] + spots[:1]
+    spots = [((x + i) % NX, (z + j) % NZ) for i in (2, 1, 3, 0) for j in (2, 1, 3, 0)]
     near = NX * NZ - 1
     has_left, has_right = t > 0, t < TILES - 1
 
@@ -181,7 +200,13 @@
     lane = lax.broadcasted_iota(jnp.int32, (8, W), 1)
     outer = (lane < W // 4) | (lane >= 3 * W // 4)
     turned = pltpu.roll(field[1, x, z, c], W // 2, axis=1)
-    packed[...] = jnp.where(outer, field[0, x, z, c], turned)
+    packed = jnp.where(outer, field[0, x, z, c], turned)
+    packed_right[...] = fold(packed, True)
+    packed_left[...] = fold(packed, False)
+    for load in small:
+        load.wait()
+    prepare_taps(khv, th)
+    prepare_taps(kvv, tv)
     count = near + 1 + len(spots) * (has_left.astype(jnp.int32) + has_right.astype(jnp.int32))
     pl.semaphore_wait(barrier, count)
 
@@ -189,8 +214,8 @@
     mains = [remote(mine, mine, es.at[d], er.at[d], at(t, *spots[d], c)) for d in range(near)]
     n = len(spots)
     slot = x * NZ + z
-    to_right = [remote(packed, left.at[slot], ss.at[d], sr.at[d], at(t + 1, *spots[d], c)) for d in range(n)]
-    to_left = [remote(packed, right.at[slot], ss.at[n + d], sr.at[n + d], at(t - 1, *spots[d], c)) for d in range(n)]
+    to_right = [remote(packed_left, left.at[slot], ss.at[d], sr.at[d], at(t + 1, *spots[d], c)) for d in range(n)]
+    to_left = [remote(packed_right, right.at[slot], ss.at[n + d], sr.at[n + d], at(t - 1, *spots[d], c)) for d in range(n)]
     @pl.when(has_right)
     def _():
         for copy in to_right:
@@ -204,10 +229,6 @@
     for copy in mains:
         copy.start()
 
-    for load in small:
-        load.wait()
-    prepare_taps(khv, th)
-    prepare_taps(kvv, tv)
     build_bands(offsets, th, tv, hf, hb, vf, vb)
     for copy in mains:
         copy.wait_recv()
@@ -227,11 +248,11 @@
         for copy in to_left:
             copy.wait_recv()
 
-    lane = lax.broadcasted_iota(jnp.int32, (n, 8, W), 2)
-    from_right_side = (lane // (W // 4)) % 2 == 0
     low = jnp.where(has_right, right[...], 0.0)
     high = jnp.where(has_left, left[...], 0.0)
-    sides[:, :, c] = jnp.where(from_right_side, low, high).reshape(NX, NZ, 8, W)
+    mask = right_lanes((n, 4, W))
+    sides[:, :, c, 0:4] = jnp.where(mask, low, high).reshape(NX, NZ, 4, W)
+    sides[:, :, c, 4:8] = jnp.where(mask, unfold(low, True), unfold(high, False)).reshape(NX, NZ, 4, W)
     rows = sides.at[:, :, c]
     swap_sides = remote(rows, rows, cs.at[1], cr.at[1], at(t, x, z, 1 - c))
     swap_sides.start()
@@ -244,25 +265,25 @@
             af[b, k] = mm3(parts[b], both(hf, b, k, 0))
         return carry
 
-    lax.fori_loop(0, NBASIS, own_columns, 0)
+    lax.fori_loop(0, NBASIS, own_columns, 0, unroll=True)
     swap_sides.wait_recv()
-    beside = split2(sides[...].reshape(ROWS, W))
+    side_parts = split2(sides[...].reshape(ROWS, W))
 
     def side_columns(k, carry):
         for b in range(BANDS):
-            a = split2(af[b, k] + mm3(beside, both(hf, b, k, 1)))
+            a = split2(af[b, k] + mm3(side_parts, both(hf, b, k, 1)))
             for part in range(2):
                 for e in range(LOCAL):
                     am[part, b, e, k] = a[part][:, e * W : (e + 1) * W]
         return carry
 
-    lax.fori_loop(0, NBASIS, side_columns, 0)
+    lax.fori_loop(0, NBASIS, side_columns, 0, unroll=True)
 
     depth = LOCAL * NBASIS * W
     shape = grad.shape[1:]
 
-    def across(b, lo):
-        h = [hb[part, b, :, :, :, lo : lo + W].reshape(depth, W) for part in range(2)]
+    def across(b):
+        h = [hb[part, b].reshape(depth, 2 * W) for part in range(2)]
         p = [jnp.concatenate([pm[part, i] for i in range(LOCAL * NBASIS)], axis=1) for part in range(2)]
         return mm3(p, h)
 
@@ -296,7 +317,8 @@
             return carry
 
         lax.fori_loop(0, LOCAL, epoch_step, 0)
-        edge = across(b, W)
+        full = across(b)
+        edge = full[:, W : 2 * W]
 
         @pl.when(b == 0)
         def _():
@@ -308,19 +330,22 @@
             grad[BANDS] = jnp.where(wide, first, pltpu.roll(edge, W // 2, axis=1)).reshape(shape)
             sum_copy(BANDS).start()
 
-        grad[b] = across(b, 0).reshape(shape)
+        grad[b] = full[:, 0:W].reshape(shape)
         sum_copy(b).start()
         return carry
 
     lax.fori_loop(0, BANDS, band_step, 0)
     take_sum(BANDS)
+    strips = half[BANDS].reshape(n, 8, W)
+    half_right[...] = fold(strips, True).reshape(NX, NZ, 4, W)
+    half_left[...] = fold(strips, False).reshape(NX, NZ, 4, W)
     to_right2 = [
-        remote(half.at[2, spots[d][0], spots[d][1]], from_left.at[slot], ss2.at[d], sr2.at[d], at(t + 1, *spots[d], c))
+        remote(half_right.at[spots[d][0], spots[d][1]], from_left.at[slot], ss2.at[d], sr2.at[d], at(t + 1, *spots[d], c))
         for d in range(n)
     ]
     to_left2 = [
         remote(
-            half.at[2, spots[d][0], spots[d][1]], from_right.at[slot], ss2.at[n + d], sr2.at[n + d], at(t - 1, *spots[d], c)
+            half_left.at[spots[d][0], spots[d][1]], from_right.at[slot], ss2.at[n + d], sr2.at[n + d], at(t - 1, *spots[d], c)
         )
         for d in range(n)
     ]
@@ -368,9 +393,11 @@
     lane = lax.broadcasted_iota(jnp.int32, (8, W), 1)
     lower = jnp.where(has_left, jnp.sum(from_left[...], axis=0), 0.0)
     upper = jnp.where(has_right, jnp.sum(from_right[...], axis=0), 0.0)
-    beside = jnp.where((lane // (W // 4)) % 2 == 0, lower, upper)
+    mask = right_lanes((4, W))
+    beside[0:4] = jnp.where(mask, lower, upper)
+    beside[4:8] = jnp.where(mask, unfold(lower, True), unfold(upper, False))
     for b in range(BANDS):
-        add = beside if b == 0 else pltpu.roll(beside, W // 2, axis=1)
+        add = beside[...] if b == 0 else pltpu.roll(beside[...], W // 2, axis=1)
         out[b] = half[b, x, z] + jnp.sum(from_e[b], axis=0) + jnp.where(outer, add, 0.0)
 
 
@@ -383,16 +410,19 @@
     n = NX * NZ
     scratch = [
         pltpu.VMEM((BANDS, *chips, NC) + tile, F32),
-        pltpu.VMEM(tile, F32),
+        pltpu.VMEM((4, W), F32),
+        pltpu.VMEM((4, W), F32),
         pltpu.VMEM((*chips, NC) + tile, F32),
-        pltpu.VMEM((n,) + tile, F32),
-        pltpu.VMEM((n,) + tile, F32),
+        pltpu.VMEM((n, 4, W), F32),
+        pltpu.VMEM((n, 4, W), F32),
         pltpu.VMEM((BANDS + 1, *chips, NC) + tile, F32),
         pltpu.VMEM((BANDS + 1, *chips) + tile, F32),
         pltpu.VMEM((BANDS + 1, *chips) + tile, F32),
         pltpu.VMEM((BANDS, n - 1) + tile, F32),
-        pltpu.VMEM((n,) + tile, F32),
-        pltpu.VMEM((n,) + tile, F32),
+        pltpu.VMEM((*chips, 4, W), F32),
+        pltpu.VMEM((*chips, 4, W), F32),
+        pltpu.VMEM((n, 4, W), F32),
+        pltpu.VMEM((n, 4, W), F32),
         pltpu.VMEM((LOCAL, NBASIS, BANDS, TAPS), F32),
         pltpu.VMEM((LOCAL, NBASIS, BANDS, TAPS), F32),
         pltpu.VMEM(coeffs.shape, BF16),
@@ -409,6 +439,7 @@
         pltpu.VMEM((BANDS, NBASIS, ROWS, LOCAL * W), F32),
         pltpu.VMEM((2, BANDS, LOCAL, NBASIS, ROWS, W), BF16),
         pltpu.VMEM((2, LOCAL * NBASIS, ROWS, W), BF16),
+        pltpu.VMEM(tile, F32),
         dma((8,)),
         dma((n - 1,)), dma((n - 1,)), dma((2 * n,)), dma((2 * n,)), dma((2,)), dma((2,)),
         dma((BANDS, n - 1)), dma((BANDS, n - 1)), dma((2 * n,)), dma((2 * n,)), dma((BANDS + 1,)), dma((BANDS + 1,)),

time: 44.9 us -> 38.7 us (0.86)
  Pallas kernels: 43.4 us -> 36.9 us
    pallas_call x1, Pallas kernels: 43.4 us -> 36.9 us  [per_device(): pl.pallas_call(kernel, out_shape=jax.ShapeDtypeStruct(scene.shape, F32),...]
where the time goes in v3:
time: 38.7 us; the launch traced here: 38.2 us
  Pallas kernels  36.9 us (95%)
  local copies, waits for them, and re-layouts  1.3 us (3%)
    pallas_call x1, Pallas kernels, per_device(): pl.pallas_call(kernel, out_shape=jax.ShapeDtypeStruct(scene.shape, F32),...  36.9 us
    unnamed x1, local copies, waits for them, and re-layouts  1.3 us

profile of v3, /device:TPU:1, one launch (start us, length us, event | category | flops | bytes accessed | tf_op | source)
XLA Modules:
  0.0 38.2 jit_solution(16751230170616285986)
XLA Ops:
  0.0 36.9 %shard_map.82 = f32[2,8,128]{2,1,0:T(8,128)} custom-call(f32[2,8,128]{2,1,0:T(8,128)} %scene.1, f32[2,5,2,21]{3,2,1,0:T(2,128)} %bitcast.3, f32[2,5,2,21]{3,2,1,0:T(2,128)} %bitcast.4, bf16[2,5,256,128]{3,2,1,0:T(8,128)(2,1)} %coeffs.1, bf16[2,2,256,128]{3,2,1,0:T(8,128)(2,1)} %observed.1, s32[2,256,128]{2,1,0:T(8,128)} %good.1, s32[1,2]{1,0:T(1,128)} %bitcast.5, ...), custom_call_target="tpu_custom_call" | custom-call | tf_op jit(solution)/shard_map/pallas_call | solution.py:447
  36.9 1.3 %copy.10 = f32[2,8,128]{2,1,0:T(8,128)} copy(f32[2,8,128]{2,1,0:T(8,128)} %shard_map.82) | data formatting | bytes 16384

commit v4 on v3

--- a/solution.py
+++ b/solution.py
@@ -8,7 +8,10 @@
 BANDS, NBASIS, TAPS = 2, 5, 21
 LOCAL = 2
 ROWS, W, TILES = 256, 128, 8
-HALF = 128
+BLOCK = 64
+EDGE = 18
+STEP = 2 * EDGE + 1
+PAD = 32
 REACH = 10
 NX, NZ, NC = 4, 4, 2
 F32, BF16 = jnp.float32, jnp.bfloat16
@@ -42,68 +45,82 @@
     lax.fori_loop(0, LOCAL * BANDS, step, 0)
 
 
-def build_bands(offsets, th, tv, hf, hb, vf, vb):
+def build_bands(offsets, th, tv, hf, hs, hb, vf, vb):
     row = lax.broadcasted_iota(jnp.int32, (W, W), 0)
     lane = lax.broadcasted_iota(jnp.int32, (W, W), 1)
     near = jnp.abs(row - lane) < W // 2
 
-    def circulant(taps, flipped, e, b, k, shift):
+    def shifted(taps, flipped, e, b, k, shift, rows):
         base = jnp.broadcast_to(taps[flipped, e, b, pl.ds(k, 1), :], (8, W))
         for bit in (1, 2, 4):
             base = jnp.where((row[0:8] & bit) != 0, pltpu.roll(base, bit, axis=1), base)
         base = pltpu.roll(base, shift, axis=1)
-        full = jnp.concatenate([base] + [pltpu.roll(base, g, axis=1) for g in range(8, W, 8)], axis=0)
+        return jnp.concatenate([base] + [pltpu.roll(base, g, axis=1) for g in range(8, rows, 8)], axis=0)
+
+    def circulant(taps, flipped, e, b, k, shift):
+        full = shifted(taps, flipped, e, b, k, shift, W)
         return split2(jnp.where(near, full, 0.0)), split2(jnp.where(near, 0.0, full))
 
     def step(i, carry):
         b, k = i // NBASIS, i % NBASIS
-        first = pl.ds(pl.multiple_of(b * (W // 2), W // 2), W // 2)
-        second = pl.ds(pl.multiple_of((1 - b) * (W // 2), W // 2), W // 2)
         for e in range(LOCAL):
             dy, dx = offsets[e, 0, 0], offsets[e, 0, 1]
             cols = slice(e * W, (e + 1) * W)
             main, edge = circulant(th, 1, e, b, k, W - REACH - dx)
             for part in range(2):
-                hf[part, b, k, 0, :, cols] = main[part]
-                hf[part, b, k, 1, first, cols] = edge[part][0 : W // 2]
-                hf[part, b, k, 1, second, cols] = edge[part][W // 2 : W]
+                hf[part, b, k, :, cols] = main[part]
+            hi, lo = edge[0].astype(F32), edge[1].astype(F32)
+            mixed = hi + pltpu.roll(hi, STEP, axis=0) + pltpu.roll(lo, 2 * STEP, axis=0)
+            hs[b, k, :, cols] = mixed.astype(BF16)
             main, edge = circulant(th, 0, e, b, k, W - REACH + dx)
             for part in range(2):
                 hb[part, b, e, k, :, 0:W] = main[part]
                 hb[part, b, e, k, :, W : 2 * W] = edge[part]
-            main, edge = circulant(tv, 0, e, b, k, W - REACH + dy)
-            for part in range(2):
-                vf[part, b, e, k, :, 0:W] = main[part]
-                vf[part, b, e, k, :, W : 2 * W] = edge[part]
-            main, edge = circulant(tv, 1, e, b, k, W - REACH - dy)
-            for part in range(2):
-                vb[part, b, e, k, :, 0:W] = main[part]
-                vb[part, b, e, k, :, W : 2 * W] = edge[part]
+            for ref, flipped, shift in ((vf, 0, PAD - REACH + dy), (vb, 1, PAD - REACH - dy)):
+                parts = split2(shifted(tv, flipped, e, b, k, shift, BLOCK))
+                for part in range(2):
+                    ref[part, b, e, k] = parts[part]
         return carry
 
     lax.fori_loop(0, BANDS * NBASIS, step, 0)
 
 
-def blocks(top, bottom):
-    zero = jnp.zeros((HALF // 2, W), BF16)
-    left = jnp.concatenate([top, bottom[0 : HALF // 2], zero], axis=0)
-    right = jnp.concatenate([bottom, zero, top[HALF // 2 : HALF]], axis=0)
-    return jnp.concatenate([left, right], axis=1)
+def blocks(parts):
+    zero = jnp.zeros((PAD, W), BF16)
+    columns = []
+    for first in range(0, ROWS, BLOCK):
+        rows = []
+        for part in parts:
+            inner = part[max(first - PAD, 0) : min(first + BLOCK + PAD, ROWS)]
+            rows += [zero] * (first == 0) + [inner] + [zero] * (first + BLOCK == ROWS)
+        columns.append(jnp.concatenate(rows, axis=0))
+    return jnp.concatenate(columns, axis=1)
 
 
 def side(value):
-    return jnp.concatenate([value[0:HALF], value[HALF:ROWS]], axis=1)
+    return jnp.concatenate([value[i : i + BLOCK] for i in range(0, ROWS, BLOCK)], axis=1)
+
+
+def upright(value):
+    return jnp.concatenate([value[:, i : i + W] for i in range(0, value.shape[1], W)], axis=0)
+
+
+def vertical(taps, parts):
+    tall = mm(jnp.concatenate([jnp.concatenate([t, t], axis=1) for t in taps], axis=0), blocks(parts))
+    return tall[0:BLOCK] + tall[BLOCK : 2 * BLOCK]
+
+
+def packed_parts(value, lane, b):
+    if b == 1:
+        value = pltpu.roll(value, W // 2, axis=1)
+    value = jnp.where((lane < EDGE) | (lane >= W - EDGE), value, 0.0)
+    hi = value.astype(BF16).astype(F32)
+    mixed = hi + pltpu.roll(value - hi, STEP, axis=1) + pltpu.roll(hi, 2 * STEP, axis=1)
+    return mixed.astype(BF16)
 
 
 def mm3(a, b):
-    if a[0].shape[1] < 2 * W:
-        wide = mm(jnp.concatenate(a, axis=1), jnp.concatenate([b[0], b[0]], axis=0))
-        return wide + mm(a[0], b[1])
-    if a[0].shape[1] > 2 * W:
-        return mm(a[0], b[0]) + mm(a[1], b[0]) + mm(a[0], b[1])
-    rows = a[0].shape[0]
-    tall = mm(jnp.concatenate(a, axis=0), b[0])
-    return tall[0:rows] + tall[rows:] + mm(a[0], b[1])
+    return mm(a[0], b[0]) + mm(a[1], b[0]) + mm(a[0], b[1])
 
 
 def both(ref, *index):
@@ -111,19 +128,16 @@
 
 
 def epoch_terms(b, e, coverage, cv, ov, gv, vf, vb, am, pm):
-    model = jnp.zeros((HALF, 2 * W), F32)
+    model = jnp.zeros((BLOCK, ROWS // BLOCK * W), F32)
     for k in range(NBASIS):
-        rows = [blocks(am[part, b, e, k, 0:HALF], am[part, b, e, k, HALF:ROWS]) for part in range(2)]
-        model = model + side(cv[e, k]).astype(F32) * mm3(both(vf, b, e, k), rows)
+        down = vertical(both(vf, b, e, k), both(am, b, e, k))
+        model = model + side(cv[e, k]).astype(F32) * down
     weight = (side(gv[e]) * coverage[0, e]).astype(F32)
     residual = weight * (model - side(ov[e, b]).astype(F32))
     for k in range(NBASIS):
-        q = split2(side(cv[e, k]).astype(F32) * residual)
-        rows = [blocks(part[:, 0:W], part[:, W : 2 * W]) for part in q]
-        up = mm3(both(vb, b, e, k), rows)
-        for part, p in enumerate(split2(up)):
-            pm[part, e * NBASIS + k, 0:HALF] = p[:, 0:W]
-            pm[part, e * NBASIS + k, HALF:ROWS] = p[:, W : 2 * W]
+        q = split2(upright(side(cv[e, k]).astype(F32) * residual))
+        for part, p in enumerate(split2(vertical(both(vb, b, e, k), q))):
+            pm[part, e * NBASIS + k] = upright(p)
 
 
 def right_lanes(shape):
@@ -145,7 +159,7 @@
 def kernel(
     scene, kh, kv, coeffs, observed, good, coverage_in, offsets_in, out,
     field, packed_right, packed_left, sides, left, right, grad, from_core, half, from_e, half_right, half_left, from_left, from_right,
-    khv, kvv, cv, ov, gv, coverage, offsets, th, tv, hf, hb, vf, vb, af, am, pm, beside,
+    khv, kvv, cv, ov, gv, coverage, offsets, th, tv, hf, hs, hb, vf, vb, am, pm, beside,
     local_sem, es, er, ss, sr, cs, cr, es2, er2, ss2, sr2, cs2, cr2,
 ):
     t, me = lax.axis_index("tile"), lax.axis_index("epoch")
@@ -169,6 +183,7 @@
     barrier = pltpu.get_barrier_semaphore()
     own = pltpu.make_async_copy(scene, field.at[:, x, z, c], local_sem.at[0])
     own.start()
+
     @pl.when(has_right)
     def _():
         for xx, zz in spots:
@@ -216,6 +231,7 @@
     slot = x * NZ + z
     to_right = [remote(packed_left, left.at[slot], ss.at[d], sr.at[d], at(t + 1, *spots[d], c)) for d in range(n)]
     to_left = [remote(packed_right, right.at[slot], ss.at[n + d], sr.at[n + d], at(t - 1, *spots[d], c)) for d in range(n)]
+
     @pl.when(has_right)
     def _():
         for copy in to_right:
@@ -229,7 +245,7 @@
     for copy in mains:
         copy.start()
 
-    build_bands(offsets, th, tv, hf, hb, vf, vb)
+    build_bands(offsets, th, tv, hf, hs, hb, vf, vb)
     for copy in mains:
         copy.wait_recv()
     rows = field.at[:, :, :, c]
@@ -259,25 +275,18 @@
 
     swap.wait_recv()
     parts = [split2(field[b].reshape(ROWS, W)) for b in range(BANDS)]
-
-    def own_columns(k, carry):
-        for b in range(BANDS):
-            af[b, k] = mm3(parts[b], both(hf, b, k, 0))
-        return carry
-
-    lax.fori_loop(0, NBASIS, own_columns, 0, unroll=True)
     swap_sides.wait_recv()
-    side_parts = split2(sides[...].reshape(ROWS, W))
-
-    def side_columns(k, carry):
-        for b in range(BANDS):
-            a = split2(af[b, k] + mm3(side_parts, both(hf, b, k, 1)))
+    beyond = sides[...].reshape(ROWS, W)
+    lane = lax.broadcasted_iota(jnp.int32, (ROWS, W), 1)
+    for b in range(BANDS):
+        hi, lo = parts[b]
+        x_all = jnp.concatenate([hi, lo, hi, packed_parts(beyond, lane, b)], axis=1)
+        for k in range(NBASIS):
+            h_all = jnp.concatenate([hf[0, b, k], hf[0, b, k], hf[1, b, k], hs[b, k]], axis=0)
+            a = split2(mm(x_all, h_all))
             for part in range(2):
                 for e in range(LOCAL):
                     am[part, b, e, k] = a[part][:, e * W : (e + 1) * W]
-        return carry
-
-    lax.fori_loop(0, NBASIS, side_columns, 0, unroll=True)
 
     depth = LOCAL * NBASIS * W
     shape = grad.shape[1:]
@@ -432,11 +441,11 @@
         pltpu.SMEM(offsets.shape, jnp.int32),
         pltpu.VMEM((2, LOCAL, BANDS, 8, W), F32),
         pltpu.VMEM((2, LOCAL, BANDS, 8, W), F32),
-        pltpu.VMEM((2, BANDS, NBASIS, 2, W, LOCAL * W), BF16),
+        pltpu.VMEM((2, BANDS, NBASIS, W, LOCAL * W), BF16),
+        pltpu.VMEM((BANDS, NBASIS, W, LOCAL * W), BF16),
         pltpu.VMEM((2, BANDS, LOCAL, NBASIS, W, 2 * W), BF16),
-        pltpu.VMEM((2, BANDS, LOCAL, NBASIS, HALF, 2 * HALF), BF16),
-        pltpu.VMEM((2, BANDS, LOCAL, NBASIS, HALF, 2 * HALF), BF16),
-        pltpu.VMEM((BANDS, NBASIS, ROWS, LOCAL * W), F32),
+        pltpu.VMEM((2, BANDS, LOCAL, NBASIS, BLOCK, W), BF16),
+        pltpu.VMEM((2, BANDS, LOCAL, NBASIS, BLOCK, W), BF16),
         pltpu.VMEM((2, BANDS, LOCAL, NBASIS, ROWS, W), BF16),
         pltpu.VMEM((2, LOCAL * NBASIS, ROWS, W), BF16),
         pltpu.VMEM(tile, F32),

time: 38.7 us -> 37.4 us (0.966)
  Pallas kernels: 36.9 us -> 35.7 us
    pallas_call x1, Pallas kernels: 36.9 us -> 35.7 us  [per_device(): pl.pallas_call(kernel, out_shape=jax.ShapeDtypeStruct(scene.shape, F32),...]
where the time goes in v4:
time: 37.4 us; the launch traced here: 37 us
  Pallas kernels  35.7 us (95%)
  local copies, waits for them, and re-layouts  1.3 us (3%)
    pallas_call x1, Pallas kernels, per_device(): pl.pallas_call(kernel, out_shape=jax.ShapeDtypeStruct(scene.shape, F32),...  35.7 us
    unnamed x1, local copies, waits for them, and re-layouts  1.3 us

profile of v4, /device:TPU:1, one launch (start us, length us, event | category | flops | bytes accessed | tf_op | source)
XLA Modules:
  0.0 37.0 jit_solution(13972001613227584212)
XLA Ops:
  0.0 35.7 %shard_map.82 = f32[2,8,128]{2,1,0:T(8,128)} custom-call(f32[2,8,128]{2,1,0:T(8,128)} %scene.1, f32[2,5,2,21]{3,2,1,0:T(2,128)} %bitcast.3, f32[2,5,2,21]{3,2,1,0:T(2,128)} %bitcast.4, bf16[2,5,256,128]{3,2,1,0:T(8,128)(2,1)} %coeffs.1, bf16[2,2,256,128]{3,2,1,0:T(8,128)(2,1)} %observed.1, s32[2,256,128]{2,1,0:T(8,128)} %good.1, s32[1,2]{1,0:T(1,128)} %bitcast.5, ...), custom_call_target="tpu_custom_call" | custom-call | tf_op jit(solution)/shard_map/pallas_call | solution.py:456
  35.7 1.3 %copy.10 = f32[2,8,128]{2,1,0:T(8,128)} copy(f32[2,8,128]{2,1,0:T(8,128)} %shard_map.82) | data formatting | bytes 16384

commit v5 on v4

--- a/solution.py
+++ b/solution.py
@@ -9,6 +9,7 @@
 LOCAL = 2
 ROWS, W, TILES = 256, 128, 8
 BLOCK = 64
+AHEAD = 4
 EDGE = 18
 STEP = 2 * EDGE + 1
 PAD = 32
@@ -45,7 +46,7 @@
     lax.fori_loop(0, LOCAL * BANDS, step, 0)
 
 
-def build_bands(offsets, th, tv, hf, hs, hb, vf, vb):
+def build_bands(lo, hi, offsets, th, tv, hf, hs, hb, vf, vb):
     row = lax.broadcasted_iota(jnp.int32, (W, W), 0)
     lane = lax.broadcasted_iota(jnp.int32, (W, W), 1)
     near = jnp.abs(row - lane) < W // 2
@@ -82,7 +83,7 @@
                     ref[part, b, e, k] = parts[part]
         return carry
 
-    lax.fori_loop(0, BANDS * NBASIS, step, 0)
+    lax.fori_loop(lo, hi, step, 0)
 
 
 def blocks(parts):
@@ -120,7 +121,9 @@
 
 
 def mm3(a, b):
-    return mm(a[0], b[0]) + mm(a[1], b[0]) + mm(a[0], b[1])
+    rows = a[0].shape[0]
+    tall = mm(jnp.concatenate(a, axis=0), b[0])
+    return tall[0:rows] + tall[rows:] + mm(a[0], b[1])
 
 
 def both(ref, *index):
@@ -222,6 +225,7 @@
         load.wait()
     prepare_taps(khv, th)
     prepare_taps(kvv, tv)
+    build_bands(0, AHEAD, offsets, th, tv, hf, hs, hb, vf, vb)
     count = near + 1 + len(spots) * (has_left.astype(jnp.int32) + has_right.astype(jnp.int32))
     pl.semaphore_wait(barrier, count)
 
@@ -245,7 +249,7 @@
     for copy in mains:
         copy.start()
 
-    build_bands(offsets, th, tv, hf, hs, hb, vf, vb)
+    build_bands(AHEAD, BANDS * NBASIS, offsets, th, tv, hf, hs, hb, vf, vb)
     for copy in mains:
         copy.wait_recv()
     rows = field.at[:, :, :, c]

time: 37.4 us -> 37.4 us (level)
  no operation moved by 1% of the time
where the time goes in v5:
time: 37.4 us; the launch traced here: 37 us
  Pallas kernels  35.7 us (95%)
  local copies, waits for them, and re-layouts  1.3 us (3%)
    pallas_call x1, Pallas kernels, per_device(): pl.pallas_call(kernel, out_shape=jax.ShapeDtypeStruct(scene.shape, F32),...  35.7 us
    unnamed x1, local copies, waits for them, and re-layouts  1.3 us

profile of v5, /device:TPU:1, one launch (start us, length us, event | category | flops | bytes accessed | tf_op | source)
XLA Modules:
  0.0 37.0 jit_solution(1278901951314577635)
XLA Ops:
  0.0 35.7 %shard_map.82 = f32[2,8,128]{2,1,0:T(8,128)} custom-call(f32[2,8,128]{2,1,0:T(8,128)} %scene.1, f32[2,5,2,21]{3,2,1,0:T(2,128)} %bitcast.3, f32[2,5,2,21]{3,2,1,0:T(2,128)} %bitcast.4, bf16[2,5,256,128]{3,2,1,0:T(8,128)(2,1)} %coeffs.1, bf16[2,2,256,128]{3,2,1,0:T(8,128)(2,1)} %observed.1, s32[2,256,128]{2,1,0:T(8,128)} %good.1, s32[1,2]{1,0:T(1,128)} %bitcast.5, ...), custom_call_target="tpu_custom_call" | custom-call | tf_op jit(solution)/shard_map/pallas_call | solution.py:460
  35.7 1.3 %copy.10 = f32[2,8,128]{2,1,0:T(8,128)} copy(f32[2,8,128]{2,1,0:T(8,128)} %shard_map.82) | data formatting | bytes 16384
